TPU v7x, 512 devices: a whole 4x4x16 slice. The times are simulated.
512 devices in a mesh: sec: 2 (over y_hi), slab: 64 (over x, z), col: 4 (over y_lo, core).
Axes of the slice: x: 4, y: 4 (y_hi: 2, y_lo: 2; y = y_hi * 2 + y_lo), z: 16, core: 2. Of those that a mesh axis runs over, the one named last changes fastest.
Arguments:
- volume: float32 [2, 20, 512, 32, 256], P('sec', None, 'slab', 'col'), may hold values from -4 to 4, as said below
- epi_line: int32 [64, 4, 64], P('slab', 'col'), may hold values from 0 to 63
- epi_dest: int32 [64, 4, 64, 1], P('slab', 'col'), may hold values from 0 to 63, as said below
- epi_target: int32 [64, 4, 64], P('slab', 'col'), may hold values from 0 to 319
Outputs:
- volume_next: float32 [2, 20, 512, 32, 256], P('sec', None, 'slab', 'col')
Inputs may be any that keep to these rules, and one draw needn't show every extreme that they name: `epi_dest`: in each heart block of 64 rows (slab s, one col) every named torso slab is named by exactly 2 rows. `volume`: gates lie in (0, 1); conductivities and reaction terms are positive.
All inputs are finite; a program needn't handle non-finite values.
Results may differ from a plain program's by a relative error of at most 0.0001.
Values sent between devices are 32-bit elements; how exact they have to be, the bound alone decides.
A program may use at most 64 MiB of HBM per device.

v0:
```python
import jax
import jax.numpy as jnp
import numpy as np
from jax import lax
from jax.sharding import PartitionSpec as P

STEPS = 4
CAP = 2


gate_half = np.linspace(-1.5, 1.5, 18).reshape(18, 1, 1, 1).astype(np.float32)
gate_slope = (0.3 + 0.1 * (np.arange(18) % 4)).reshape(18, 1, 1, 1).astype(np.float32)
gate_decay = (
    np.exp(-1.0 / (2.0 * 30.0 ** (np.arange(18) / 17.0))).reshape(18, 1, 1, 1).astype(np.float32)
)
gate_conduct = (0.02 + 0.01 * (np.arange(18) % 3)).reshape(18, 1, 1, 1).astype(np.float32)
gate_reversal = np.linspace(-1.0, 1.0, 18).reshape(18, 1, 1, 1).astype(np.float32)
relax_omega = 1.5625


def extended(cells, sides, width):
    for axis, dim in sides:
        count = lax.axis_size(axis)
        ends = count - 1
        head = lax.slice_in_dim(cells, 0, width, axis=dim)
        tail = lax.slice_in_dim(cells, cells.shape[dim] - width, cells.shape[dim], axis=dim)
        cells = jnp.concatenate(
            [
                lax.ppermute(tail, axis, [(i, (i + 1) % count) for i in range(ends)]),
                cells,
                lax.ppermute(head, axis, [((i + 1) % count, i) for i in range(ends)]),
            ],
            axis=dim,
        )
    return cells


def ionic(volts, gates, sigma, lap_x, lap_y, lap_z):
    steady = jax.nn.sigmoid((volts[None] - gate_half) / gate_slope)
    gates = steady + (gates - steady) * gate_decay
    current = jnp.sum(gate_conduct * gates * (volts[None] - gate_reversal), axis=0)
    volts = volts + sigma * (0.12 * lap_x + 0.04 * lap_y + 0.04 * lap_z) - current
    return (volts, gates)


def on_device(volume, epi_line, epi_dest, epi_target):
    block = volume[0]
    width_x, width_y, width_z = (block.shape[1], block.shape[2], block.shape[3])
    slab_count = lax.axis_size("slab")
    is_heart = lax.axis_index("sec") == 0
    slab_index = lax.axis_index("slab")
    col_index = lax.axis_index("col")
    first_slab = slab_index == 0
    last_slab = slab_index == slab_count - 1
    first_col = col_index == 0
    last_col = col_index == lax.axis_size("col") - 1

    def heart_faces(state):
        volts = state[0]
        faces_along = jnp.stack([volts[0], volts[-1]], axis=0)
        faces_across = jnp.stack([volts[:, 0], volts[:, -1]], axis=0)
        faces_across = jnp.pad(faces_across, ((0, 0), (0, 4 * width_x), (0, 0)))
        return (faces_along, faces_across)

    def torso_faces(state):
        potential = state.reshape(4, 5 * width_x, width_y, width_z)[0]
        faces_along = jnp.stack([potential[0], potential[-1]], axis=0)
        faces_across = jnp.stack([potential[:, 0], potential[:, -1]], axis=0)
        return (faces_along, faces_across)

    def heart_update(state, halo_along, halo_across):
        volts = state[0]
        low_x = jnp.where(first_slab, volts[0], halo_along[0])
        high_x = jnp.where(last_slab, volts[-1], halo_along[3])
        low_y = jnp.where(first_col, volts[:, 0], halo_across[0, :width_x])
        high_y = jnp.where(last_col, volts[:, -1], halo_across[3, :width_x])
        along_x = jnp.concatenate([low_x[None], volts, high_x[None]], axis=0)
        along_y = jnp.concatenate([low_y[:, None], volts, high_y[:, None]], axis=1)
        along_z = jnp.concatenate([volts[:, :, :1], volts, volts[:, :, -1:]], axis=2)
        lap_x = along_x[2:] + along_x[:-2] - 2.0 * volts
        lap_y = along_y[:, 2:] + along_y[:, :-2] - 2.0 * volts
        lap_z = along_z[:, :, 2:] + along_z[:, :, :-2] - 2.0 * volts
        volts, gates = ionic(volts, state[1:19], state[19], lap_x, lap_y, lap_z)
        return jnp.concatenate([volts[None], gates, state[19:]], axis=0)

    def torso_update(state, halo_along, halo_across):
        fields = state.reshape(4, 5 * width_x, width_y, width_z)
        potential, previous, mass_term, source = (fields[0], fields[1], fields[2], fields[3])
        along_x = jnp.concatenate([halo_along[0][None], potential, halo_along[3][None]], axis=0)
        along_y = jnp.concatenate(
            [halo_across[0][:, None], potential, halo_across[3][:, None]], axis=1
        )
        along_z = jnp.pad(potential, ((0, 0), (0, 0), (1, 1)))
        beside = along_x[2:] + along_x[:-2]
        beside = beside + along_y[:, 2:] + along_y[:, :-2]
        beside = beside + along_z[:, :, 2:] + along_z[:, :, :-2]
        applied = (6.0 + mass_term) * potential - beside
        update = (source - applied) / (6.0 + mass_term)
        fresh = previous + relax_omega * (potential + update - previous)
        return jnp.stack([fresh, potential, mass_term, source], axis=0).reshape(
            20, width_x, width_y, width_z
        )

    for step in range(STEPS):
        faces_along, faces_across = lax.cond(is_heart, heart_faces, torso_faces, block)
        halo_along = extended(faces_along, (("slab", 0),), 1)
        halo_across = extended(faces_across, (("col", 0),), 1)
        block = lax.cond(is_heart, heart_update, torso_update, block, halo_along, halo_across)
    heart_mask = is_heart.astype(jnp.float32)
    lines = block[0].reshape(width_x * width_y, width_z)
    picked = jnp.take(lines, epi_line.reshape(-1), axis=0)
    dest = epi_dest.reshape(-1)
    target = epi_target.reshape(-1)
    marks = (dest[:, None] == jnp.arange(slab_count, dtype=jnp.int32)[None, :]).astype(jnp.int32)
    slot = jnp.sum(jnp.cumsum(marks, axis=0) * marks, axis=1) - 1
    place_key = dest * CAP + slot
    total_slots = slab_count * CAP
    place = (jnp.arange(total_slots, dtype=jnp.int32)[:, None] == place_key[None, :]).astype(
        jnp.float32
    )
    send_rows = jnp.dot(place, picked, precision=lax.Precision.HIGHEST) * heart_mask
    send_lines = (
        jnp.dot(place, (target + 1).astype(jnp.float32), precision=lax.Precision.HIGHEST)
        * heart_mask
        - 1.0
    )
    rows_both = jnp.concatenate([jnp.zeros_like(send_rows), send_rows], axis=0).reshape(
        2 * slab_count, CAP, width_z
    )
    lines_both = jnp.concatenate([-jnp.ones_like(send_lines), send_lines], axis=0).reshape(
        2 * slab_count, CAP
    )
    got_rows, got_lines = (
        lax.all_to_all(rows_both, ("sec", "slab"), split_axis=0, concat_axis=0, tiled=True),
        lax.all_to_all(lines_both, ("sec", "slab"), split_axis=0, concat_axis=0, tiled=True),
    )
    got_rows = got_rows[:slab_count].reshape(total_slots, width_z)
    got_lines = got_lines[:slab_count].reshape(total_slots)
    line_count = 5 * width_x * width_y
    hits = (
        jnp.arange(line_count, dtype=jnp.int32).astype(jnp.float32)[:, None] == got_lines[None, :]
    ).astype(jnp.float32)
    inflow = jnp.dot(hits, got_rows, precision=lax.Precision.HIGHEST).reshape(
        5 * width_x, width_y, width_z
    )
    torso_fields = block.reshape(4, 5 * width_x, width_y, width_z)
    torso_out = jnp.concatenate([torso_fields[:3], inflow[None]], axis=0).reshape(
        20, width_x, width_y, width_z
    )
    result = jnp.where(is_heart, block, torso_out)
    return result[None]


def solution(mesh):
    placed = (
        P("sec", None, "slab", "col", None),
        P("slab", "col", None),
        P("slab", "col", None, None),
        P("slab", "col", None),
    )
    return jax.shard_map(
        on_device,
        mesh=mesh,
        in_specs=placed,
        out_specs=P("sec", None, "slab", "col", None),
        check_vma=False,
    )
```

profile of v0, /device:TPU:2, one launch (start us, length us, event | category | flops | bytes accessed | tf_op | source)
XLA Modules:
  0.0 127.2 jit_solution(5974312680414271014)
XLA Ops:
  0.1 1.7 %conditional.8 = (f32[2,8,256]{2,1,0:T(8,128)S(1)}, f32[2,40,256]{2,0,1:T(2,128)S(1)}) conditional(s32[]{:T(128)} %convert_element_type.41, f32[1,20,8,8,256]{4,3,2,1,0:T(8,128)} %param.25, f32[20,8,8,256]{3,2,1,0:T(8,128)} %bitcast.266), branch_computations={%region_0.0_spmd, %region_1.2_spmd} | conditional | flops 86016 | bytes 1048592 | solution.py:105
  0.1 0.9 slice_bitcast_fusion.2
  1.0 0.7 slice_bitcast_fusion.6
  1.8 1.3 %collective-permute-start.2 = (f32[1,40,256]{2,0,1:T(1,128)S(1)}, f32[1,40,256]{2,0,1:T(1,128)S(1)}, u32[]{:S(2)}, u32[]{:S(2)}) collective-permute-start(f32[1,40,256]{2,0,1:T(1,128)S(1)} %get-tuple-element.368), channel_id=1, source_target_pairs={{1,0},{2,1},{3,2},{5,4},{6,5},{7,6},{9,8},{10,9},{11,10},{13,12},{... | collective-permute-start | bytes 122888 | tf_op jit(solution)/shard_map/ppermute | solution.py:31
  3.1 3.0 %collective-permute-start.3 = (f32[1,40,256]{2,0,1:T(1,128)S(1)}, f32[1,40,256]{2,0,1:T(1,128)S(1)}, u32[]{:S(2)}, u32[]{:S(2)}) collective-permute-start(f32[1,40,256]{2,0,1:T(1,128)S(1)} %get-tuple-element.367), channel_id=1, source_target_pairs={{0,1},{1,2},{2,3},{4,5},{5,6},{6,7},{8,9},{9,10},{10,11},{12,13},{... | collective-permute-start | bytes 122888 | tf_op jit(solution)/shard_map/ppermute | solution.py:29
  6.2 11.4 %collective-permute-start = (f32[1,8,256]{2,1,0:T(8,128)S(1)}, f32[1,8,256]{2,1,0:T(8,128)S(1)}, u32[]{:S(2)}, u32[]{:S(2)}) collective-permute-start(f32[1,8,256]{2,1,0:T(8,128)S(1)} %get-tuple-element.376), channel_id=1, source_target_pairs={{4,0},{8,4},{12,8},{16,12},{20,16},{24,20},{28,24},{32,28},{36,32}... | collective-permute-start | bytes 24584 | tf_op jit(solution)/shard_map/ppermute | solution.py:31
  17.5 1.9 %collective-permute-start.1 = (f32[1,8,256]{2,1,0:T(8,128)S(1)}, f32[1,8,256]{2,1,0:T(8,128)S(1)}, u32[]{:S(2)}, u32[]{:S(2)}) collective-permute-start(f32[1,8,256]{2,1,0:T(8,128)S(1)} %get-tuple-element.375), channel_id=1, source_target_pairs={{0,4},{4,8},{8,12},{12,16},{16,20},{20,24},{24,28},{28,32},{32,36}... | collective-permute-start | bytes 24584 | tf_op jit(solution)/shard_map/ppermute | solution.py:29
  19.6 0.2 select_reduce_fusion
  19.9 0.1 fusion.97
  20.0 0.8 all_to_all.9
  20.8 14.2 %all-to-all-start = ((f32[128,1,2]{2,1,0:T(1,128)}), f32[128,1,2]{2,1,0:T(1,128)S(1)}, u32[]{:S(2)}, u32[]{:S(2)}) async-start(f32[128,1,2]{2,1,0:T(1,128)} %bitcast.130), calls=%async_computation | async-start | bytes 131072 | tf_op jit(solution)/shard_map/all_to_all | solution.py:135
  35.1 4.8 %conditional.9 = (f32[20,8,8,256]{3,2,1,0:T(8,128)S(1)}) conditional(s32[]{:T(128)} %convert_element_type.41, (f32[1,20,8,8,256]{4,3,2,1,0:T(8,128)}, f32[1,8,256]{2,1,0:T(8,128)S(1)}, f32[1,8,256]{2,1,0:T(8,128)S(1)}, f32[1,40,256]{2,0,1:T(1,128)S(1)}, f32[1,40,256]{2,0,1:T(1,128)S(1)}) %tuple.61, (f32[20,8,8,256]{3,2,1,0:T(8,128)}, pred[]{:T(512)}, ...), branch_computations={%region_2.3_spmd, %region_3.5_spmd} | conditional | flops 4530176 | bytes 7307272 | solution.py:108
  35.1 0.9 slice_bitcast_fusion.7
  36.0 2.0 %multiply_reduce_fusion = (f32[8,8,256]{2,1,0:T(8,128)S(1)}, f32[18,8,8,256]{3,2,1,0:T(8,128)S(1)}) fusion(f32[18]{0:T(128)S(1)} %bitcast.322, f32[8,8,256]{2,1,0:T(8,128)S(1)} %get-tuple-element.331, f32[18]{0:T(128)S(1)} %bitcast.318, f32[18]{0:T(128)S(1)} %bitcast.314, f32[20,8,8,256]{3,2,1,0:T(8,128)} %get-tuple-element.182, f32[18]{0:T(128)S(1)} %bitcast.310, ...), kind=kLoop, calls=%fused_computation.33 | loop fusion | flops 3522560 | bytes 2490728 | tf_op jit(solution)/shard_map/cond/branch_1_fun/reduce_sum | solution.py:41
  38.1 0.7 bitcast_select_fusion.1
  38.8 1.0 fusion.17
  40.1 1.3 %collective-permute-start.6 = (f32[1,40,256]{2,0,1:T(1,128)S(1)}, f32[1,40,256]{2,0,1:T(1,128)S(1)}, u32[]{:S(2)}, u32[]{:S(2)}) collective-permute-start(f32[1,40,256]{2,0,1:T(1,128)S(1)} %get-tuple-element.366), channel_id=1, source_target_pairs={{1,0},{2,1},{3,2},{5,4},{6,5},{7,6},{9,8},{10,9},{11,10},{13,12},{... | collective-permute-start | bytes 122888 | tf_op jit(solution)/shard_map/ppermute | solution.py:31
  41.4 3.0 %collective-permute-start.7 = (f32[1,40,256]{2,0,1:T(1,128)S(1)}, f32[1,40,256]{2,0,1:T(1,128)S(1)}, u32[]{:S(2)}, u32[]{:S(2)}) collective-permute-start(f32[1,40,256]{2,0,1:T(1,128)S(1)} %get-tuple-element.365), channel_id=1, source_target_pairs={{0,1},{1,2},{2,3},{4,5},{5,6},{6,7},{8,9},{9,10},{10,11},{12,13},{... | collective-permute-start | bytes 122888 | tf_op jit(solution)/shard_map/ppermute | solution.py:29
  44.4 4.6 %collective-permute-start.4 = (f32[1,8,256]{2,1,0:T(8,128)S(1)}, f32[1,8,256]{2,1,0:T(8,128)S(1)}, u32[]{:S(2)}, u32[]{:S(2)}) collective-permute-start(f32[1,8,256]{2,1,0:T(8,128)S(1)} %get-tuple-element.374), channel_id=1, source_target_pairs={{4,0},{8,4},{12,8},{16,12},{20,16},{24,20},{28,24},{32,28},{36,32}... | collective-permute-start | bytes 24584 | tf_op jit(solution)/shard_map/ppermute | solution.py:31
  49.0 1.9 %collective-permute-start.5 = (f32[1,8,256]{2,1,0:T(8,128)S(1)}, f32[1,8,256]{2,1,0:T(8,128)S(1)}, u32[]{:S(2)}, u32[]{:S(2)}) collective-permute-start(f32[1,8,256]{2,1,0:T(8,128)S(1)} %get-tuple-element.373), channel_id=1, source_target_pairs={{0,4},{4,8},{8,12},{12,16},{16,20},{20,24},{24,28},{28,32},{32,36}... | collective-permute-start | bytes 24584 | tf_op jit(solution)/shard_map/ppermute | solution.py:29
  51.0 5.7 %collective-permute-done.5 = f32[1,8,256]{2,1,0:T(8,128)S(1)} collective-permute-done((f32[1,8,256]{2,1,0:T(8,128)S(1)}, f32[1,8,256]{2,1,0:T(8,128)S(1)}, u32[]{:S(2)}, u32[]{:S(2)}) %collective-permute-start.5) | collective-permute-done | bytes 8224 | tf_op jit(solution)/shard_map/ppermute | solution.py:29
  56.7 1.1 conditional.11
  56.7 0.7 multiply_reduce_fusion.1
  57.5 0.1 fusion.41
  58.0 1.3 %collective-permute-start.10 = (f32[1,40,256]{2,0,1:T(1,128)S(1)}, f32[1,40,256]{2,0,1:T(1,128)S(1)}, u32[]{:S(2)}, u32[]{:S(2)}) collective-permute-start(f32[1,40,256]{2,0,1:T(1,128)S(1)} %get-tuple-element.364), channel_id=1, source_target_pairs={{1,0},{2,1},{3,2},{5,4},{6,5},{7,6},{9,8},{10,9},{11,10},{13,12},{... | collective-permute-start | bytes 122888 | tf_op jit(solution)/shard_map/ppermute | solution.py:31
  59.3 3.0 %collective-permute-start.11 = (f32[1,40,256]{2,0,1:T(1,128)S(1)}, f32[1,40,256]{2,0,1:T(1,128)S(1)}, u32[]{:S(2)}, u32[]{:S(2)}) collective-permute-start(f32[1,40,256]{2,0,1:T(1,128)S(1)} %get-tuple-element.363), channel_id=1, source_target_pairs={{0,1},{1,2},{2,3},{4,5},{5,6},{6,7},{8,9},{9,10},{10,11},{12,13},{... | collective-permute-start | bytes 122888 | tf_op jit(solution)/shard_map/ppermute | solution.py:29
  62.3 1.9 %collective-permute-start.8 = (f32[1,8,256]{2,1,0:T(8,128)S(1)}, f32[1,8,256]{2,1,0:T(8,128)S(1)}, u32[]{:S(2)}, u32[]{:S(2)}) collective-permute-start(f32[1,8,256]{2,1,0:T(8,128)S(1)} %get-tuple-element.372), channel_id=1, source_target_pairs={{4,0},{8,4},{12,8},{16,12},{20,16},{24,20},{28,24},{32,28},{36,32}... | collective-permute-start | bytes 24584 | tf_op jit(solution)/shard_map/ppermute | solution.py:31
  64.3 3.9 %collective-permute-start.9 = (f32[1,8,256]{2,1,0:T(8,128)S(1)}, f32[1,8,256]{2,1,0:T(8,128)S(1)}, u32[]{:S(2)}, u32[]{:S(2)}) collective-permute-start(f32[1,8,256]{2,1,0:T(8,128)S(1)} %get-tuple-element.371), channel_id=1, source_target_pairs={{0,4},{4,8},{8,12},{12,16},{16,20},{20,24},{24,28},{28,32},{32,36}... | collective-permute-start | bytes 24584 | tf_op jit(solution)/shard_map/ppermute | solution.py:29
  68.2 3.7 %collective-permute-done.9 = f32[1,8,256]{2,1,0:T(8,128)S(1)} collective-permute-done((f32[1,8,256]{2,1,0:T(8,128)S(1)}, f32[1,8,256]{2,1,0:T(8,128)S(1)}, u32[]{:S(2)}, u32[]{:S(2)}) %collective-permute-start.9) | collective-permute-done | bytes 8224 | tf_op jit(solution)/shard_map/ppermute | solution.py:29
  71.9 1.1 conditional.13
  71.9 0.7 multiply_reduce_fusion.2
  72.7 0.1 fusion.65
  73.2 1.3 %collective-permute-start.14 = (f32[1,40,256]{2,0,1:T(1,128)S(1)}, f32[1,40,256]{2,0,1:T(1,128)S(1)}, u32[]{:S(2)}, u32[]{:S(2)}) collective-permute-start(f32[1,40,256]{2,0,1:T(1,128)S(1)} %get-tuple-element.362), channel_id=1, source_target_pairs={{1,0},{2,1},{3,2},{5,4},{6,5},{7,6},{9,8},{10,9},{11,10},{13,12},{... | collective-permute-start | bytes 122888 | tf_op jit(solution)/shard_map/ppermute | solution.py:31
  74.5 3.0 %collective-permute-start.15 = (f32[1,40,256]{2,0,1:T(1,128)S(1)}, f32[1,40,256]{2,0,1:T(1,128)S(1)}, u32[]{:S(2)}, u32[]{:S(2)}) collective-permute-start(f32[1,40,256]{2,0,1:T(1,128)S(1)} %get-tuple-element.361), channel_id=1, source_target_pairs={{0,1},{1,2},{2,3},{4,5},{5,6},{6,7},{8,9},{9,10},{10,11},{12,13},{... | collective-permute-start | bytes 122888 | tf_op jit(solution)/shard_map/ppermute | solution.py:29
  77.5 1.9 %collective-permute-start.12 = (f32[1,8,256]{2,1,0:T(8,128)S(1)}, f32[1,8,256]{2,1,0:T(8,128)S(1)}, u32[]{:S(2)}, u32[]{:S(2)}) collective-permute-start(f32[1,8,256]{2,1,0:T(8,128)S(1)} %get-tuple-element.370), channel_id=1, source_target_pairs={{4,0},{8,4},{12,8},{16,12},{20,16},{24,20},{28,24},{32,28},{36,32}... | collective-permute-start | bytes 24584 | tf_op jit(solution)/shard_map/ppermute | solution.py:31
  79.5 3.9 %collective-permute-start.13 = (f32[1,8,256]{2,1,0:T(8,128)S(1)}, f32[1,8,256]{2,1,0:T(8,128)S(1)}, u32[]{:S(2)}, u32[]{:S(2)}) collective-permute-start(f32[1,8,256]{2,1,0:T(8,128)S(1)} %get-tuple-element.369), channel_id=1, source_target_pairs={{0,4},{4,8},{8,12},{12,16},{16,20},{20,24},{24,28},{28,32},{32,36}... | collective-permute-start | bytes 24584 | tf_op jit(solution)/shard_map/ppermute | solution.py:29
  83.4 3.7 %collective-permute-done.13 = f32[1,8,256]{2,1,0:T(8,128)S(1)} collective-permute-done((f32[1,8,256]{2,1,0:T(8,128)S(1)}, f32[1,8,256]{2,1,0:T(8,128)S(1)}, u32[]{:S(2)}, u32[]{:S(2)}) %collective-permute-start.13) | collective-permute-done | bytes 8224 | tf_op jit(solution)/shard_map/ppermute | solution.py:29
  87.1 1.1 conditional.15
  87.1 0.7 multiply_reduce_fusion.3
  87.9 0.1 fusion.89
  88.2 0.7 gather_fusion
  88.9 0.3 convolution_multiply_fusion
  89.2 0.8 reshape.204
  90.0 11.1 %all-to-all-start.1 = ((f32[128,2,256]{2,1,0:T(2,128)}), f32[128,2,256]{2,1,0:T(2,128)S(1)}, u32[]{:S(2)}, u32[]{:S(2)}) async-start(f32[128,2,256]{2,1,0:T(2,128)} %reshape.204), calls=%async_computation.1 | async-start | bytes 524288 | tf_op jit(solution)/shard_map/all_to_all | solution.py:134
  101.2 0.1 eq.73
  101.5 23.9 %all-to-all-done.1 = f32[128,2,256]{2,1,0:T(2,128)S(1)} async-done(((f32[128,2,256]{2,1,0:T(2,128)}), f32[128,2,256]{2,1,0:T(2,128)S(1)}, u32[]{:S(2)}, u32[]{:S(2)}) %all-to-all-start.1) | async-done | bytes 262176 | tf_op jit(solution)/shard_map/all_to_all | solution.py:134
  125.5 0.3 convolution_bitcast_fusion
  125.9 1.2 select_bitcast_fusion
  (92 shorter events, 2.4 us)
Async XLA Ops:
  0.0 35.0 %copy-start = (f32[18,1,1,1]{0,3,2,1:T(1,128)S(1)}, f32[18,1,1,1]{0,3,2,1:T(1,128)}, u32[]{:S(2)}) copy-start(f32[18,1,1,1]{0,3,2,1:T(1,128)} %constant.143.clone) | copy-start | bytes 220
  0.0 35.1 %copy-start.1 = (f32[18,1,1,1]{0,3,2,1:T(1,128)S(1)}, f32[18,1,1,1]{0,3,2,1:T(1,128)}, u32[]{:S(2)}) copy-start(f32[18,1,1,1]{0,3,2,1:T(1,128)} %constant.144.clone) | copy-start | bytes 220
  0.0 35.1 %copy-start.2 = (f32[18,1,1,1]{0,3,2,1:T(1,128)S(1)}, f32[18,1,1,1]{0,3,2,1:T(1,128)}, u32[]{:S(2)}) copy-start(f32[18,1,1,1]{0,3,2,1:T(1,128)} %constant.145.clone) | copy-start | bytes 220
  0.0 35.1 %copy-start.3 = (f32[18,1,1,1]{0,3,2,1:T(1,128)S(1)}, f32[18,1,1,1]{0,3,2,1:T(1,128)}, u32[]{:S(2)}) copy-start(f32[18,1,1,1]{0,3,2,1:T(1,128)} %constant.146.clone) | copy-start | bytes 220
  0.0 35.1 %copy-start.4 = (f32[18,1,1,1]{0,3,2,1:T(1,128)S(1)}, f32[18,1,1,1]{0,3,2,1:T(1,128)}, u32[]{:S(2)}) copy-start(f32[18,1,1,1]{0,3,2,1:T(1,128)} %constant.147.clone) | copy-start | bytes 220
  0.0 19.4 %copy-start.5 = (s32[1,1,64,1]{2,3,1,0:T(1,128)S(1)}, s32[1,1,64,1]{2,3,1,0:T(1,128)}, u32[]{:S(2)}) copy-start(s32[1,1,64,1]{2,3,1,0:T(1,128)} %param.27) | copy-start | bytes 772
  0.0 19.8 %copy-start.6 = (s32[1,1,64]{2,1,0:T(1,128)S(1)}, s32[1,1,64]{2,1,0:T(1,128)}, u32[]{:S(2)}) copy-start(s32[1,1,64]{2,1,0:T(1,128)} %param.28) | copy-start | bytes 772
  1.8 33.2 %collective-permute-start.2 = (f32[1,40,256]{2,0,1:T(1,128)S(1)}, f32[1,40,256]{2,0,1:T(1,128)S(1)}, u32[]{:S(2)}, u32[]{:S(2)}) collective-permute-start(f32[1,40,256]{2,0,1:T(1,128)S(1)} %get-tuple-element.368), channel_id=1, source_target_pairs={{1,0},{2,1},{3,2},{5,4},{6,5},{7,6},{9,8},{10,9},{11,10},{13,12},{... | collective-permute-start | bytes 122888 | tf_op jit(solution)/shard_map/ppermute | solution.py:31
  3.1 31.9 %collective-permute-start.3 = (f32[1,40,256]{2,0,1:T(1,128)S(1)}, f32[1,40,256]{2,0,1:T(1,128)S(1)}, u32[]{:S(2)}, u32[]{:S(2)}) collective-permute-start(f32[1,40,256]{2,0,1:T(1,128)S(1)} %get-tuple-element.367), channel_id=1, source_target_pairs={{0,1},{1,2},{2,3},{4,5},{5,6},{6,7},{8,9},{9,10},{10,11},{12,13},{... | collective-permute-start | bytes 122888 | tf_op jit(solution)/shard_map/ppermute | solution.py:29
  6.2 28.9 %collective-permute-start = (f32[1,8,256]{2,1,0:T(8,128)S(1)}, f32[1,8,256]{2,1,0:T(8,128)S(1)}, u32[]{:S(2)}, u32[]{:S(2)}) collective-permute-start(f32[1,8,256]{2,1,0:T(8,128)S(1)} %get-tuple-element.376), channel_id=1, source_target_pairs={{4,0},{8,4},{12,8},{16,12},{20,16},{24,20},{28,24},{32,28},{36,32}... | collective-permute-start | bytes 24584 | tf_op jit(solution)/shard_map/ppermute | solution.py:31
  17.5 17.5 %collective-permute-start.1 = (f32[1,8,256]{2,1,0:T(8,128)S(1)}, f32[1,8,256]{2,1,0:T(8,128)S(1)}, u32[]{:S(2)}, u32[]{:S(2)}) collective-permute-start(f32[1,8,256]{2,1,0:T(8,128)S(1)} %get-tuple-element.375), channel_id=1, source_target_pairs={{0,4},{4,8},{8,12},{12,16},{16,20},{20,24},{24,28},{28,32},{32,36}... | collective-permute-start | bytes 24584 | tf_op jit(solution)/shard_map/ppermute | solution.py:29
  20.8 69.2 %all-to-all-start = ((f32[128,1,2]{2,1,0:T(1,128)}), f32[128,1,2]{2,1,0:T(1,128)S(1)}, u32[]{:S(2)}, u32[]{:S(2)}) async-start(f32[128,1,2]{2,1,0:T(1,128)} %bitcast.130), calls=%async_computation | async-start | bytes 131072 | tf_op jit(solution)/shard_map/all_to_all | solution.py:135
  39.9 11.1 %copy-start.7 = (s32[1,1,64]{2,1,0:T(1,128)S(1)}, s32[1,1,64]{2,1,0:T(1,128)}, u32[]{:S(2)}) copy-start(s32[1,1,64]{2,1,0:T(1,128)} %param.26) | copy-start | bytes 772
  40.1 16.6 %collective-permute-start.6 = (f32[1,40,256]{2,0,1:T(1,128)S(1)}, f32[1,40,256]{2,0,1:T(1,128)S(1)}, u32[]{:S(2)}, u32[]{:S(2)}) collective-permute-start(f32[1,40,256]{2,0,1:T(1,128)S(1)} %get-tuple-element.366), channel_id=1, source_target_pairs={{1,0},{2,1},{3,2},{5,4},{6,5},{7,6},{9,8},{10,9},{11,10},{13,12},{... | collective-permute-start | bytes 122888 | tf_op jit(solution)/shard_map/ppermute | solution.py:31
  41.4 15.3 %collective-permute-start.7 = (f32[1,40,256]{2,0,1:T(1,128)S(1)}, f32[1,40,256]{2,0,1:T(1,128)S(1)}, u32[]{:S(2)}, u32[]{:S(2)}) collective-permute-start(f32[1,40,256]{2,0,1:T(1,128)S(1)} %get-tuple-element.365), channel_id=1, source_target_pairs={{0,1},{1,2},{2,3},{4,5},{5,6},{6,7},{8,9},{9,10},{10,11},{12,13},{... | collective-permute-start | bytes 122888 | tf_op jit(solution)/shard_map/ppermute | solution.py:29
  44.4 6.5 %collective-permute-start.4 = (f32[1,8,256]{2,1,0:T(8,128)S(1)}, f32[1,8,256]{2,1,0:T(8,128)S(1)}, u32[]{:S(2)}, u32[]{:S(2)}) collective-permute-start(f32[1,8,256]{2,1,0:T(8,128)S(1)} %get-tuple-element.374), channel_id=1, source_target_pairs={{4,0},{8,4},{12,8},{16,12},{20,16},{24,20},{28,24},{32,28},{36,32}... | collective-permute-start | bytes 24584 | tf_op jit(solution)/shard_map/ppermute | solution.py:31
  49.0 7.7 %collective-permute-start.5 = (f32[1,8,256]{2,1,0:T(8,128)S(1)}, f32[1,8,256]{2,1,0:T(8,128)S(1)}, u32[]{:S(2)}, u32[]{:S(2)}) collective-permute-start(f32[1,8,256]{2,1,0:T(8,128)S(1)} %get-tuple-element.373), channel_id=1, source_target_pairs={{0,4},{4,8},{8,12},{12,16},{16,20},{20,24},{24,28},{28,32},{32,36}... | collective-permute-start | bytes 24584 | tf_op jit(solution)/shard_map/ppermute | solution.py:29
  58.0 13.9 %collective-permute-start.10 = (f32[1,40,256]{2,0,1:T(1,128)S(1)}, f32[1,40,256]{2,0,1:T(1,128)S(1)}, u32[]{:S(2)}, u32[]{:S(2)}) collective-permute-start(f32[1,40,256]{2,0,1:T(1,128)S(1)} %get-tuple-element.364), channel_id=1, source_target_pairs={{1,0},{2,1},{3,2},{5,4},{6,5},{7,6},{9,8},{10,9},{11,10},{13,12},{... | collective-permute-start | bytes 122888 | tf_op jit(solution)/shard_map/ppermute | solution.py:31
  59.3 12.6 %collective-permute-start.11 = (f32[1,40,256]{2,0,1:T(1,128)S(1)}, f32[1,40,256]{2,0,1:T(1,128)S(1)}, u32[]{:S(2)}, u32[]{:S(2)}) collective-permute-start(f32[1,40,256]{2,0,1:T(1,128)S(1)} %get-tuple-element.363), channel_id=1, source_target_pairs={{0,1},{1,2},{2,3},{4,5},{5,6},{6,7},{8,9},{9,10},{10,11},{12,13},{... | collective-permute-start | bytes 122888 | tf_op jit(solution)/shard_map/ppermute | solution.py:29
  62.3 5.9 %collective-permute-start.8 = (f32[1,8,256]{2,1,0:T(8,128)S(1)}, f32[1,8,256]{2,1,0:T(8,128)S(1)}, u32[]{:S(2)}, u32[]{:S(2)}) collective-permute-start(f32[1,8,256]{2,1,0:T(8,128)S(1)} %get-tuple-element.372), channel_id=1, source_target_pairs={{4,0},{8,4},{12,8},{16,12},{20,16},{24,20},{28,24},{32,28},{36,32}... | collective-permute-start | bytes 24584 | tf_op jit(solution)/shard_map/ppermute | solution.py:31
  64.3 7.7 %collective-permute-start.9 = (f32[1,8,256]{2,1,0:T(8,128)S(1)}, f32[1,8,256]{2,1,0:T(8,128)S(1)}, u32[]{:S(2)}, u32[]{:S(2)}) collective-permute-start(f32[1,8,256]{2,1,0:T(8,128)S(1)} %get-tuple-element.371), channel_id=1, source_target_pairs={{0,4},{4,8},{8,12},{12,16},{16,20},{20,24},{24,28},{28,32},{32,36}... | collective-permute-start | bytes 24584 | tf_op jit(solution)/shard_map/ppermute | solution.py:29
  73.2 13.9 %collective-permute-start.14 = (f32[1,40,256]{2,0,1:T(1,128)S(1)}, f32[1,40,256]{2,0,1:T(1,128)S(1)}, u32[]{:S(2)}, u32[]{:S(2)}) collective-permute-start(f32[1,40,256]{2,0,1:T(1,128)S(1)} %get-tuple-element.362), channel_id=1, source_target_pairs={{1,0},{2,1},{3,2},{5,4},{6,5},{7,6},{9,8},{10,9},{11,10},{13,12},{... | collective-permute-start | bytes 122888 | tf_op jit(solution)/shard_map/ppermute | solution.py:31
  74.5 12.6 %collective-permute-start.15 = (f32[1,40,256]{2,0,1:T(1,128)S(1)}, f32[1,40,256]{2,0,1:T(1,128)S(1)}, u32[]{:S(2)}, u32[]{:S(2)}) collective-permute-start(f32[1,40,256]{2,0,1:T(1,128)S(1)} %get-tuple-element.361), channel_id=1, source_target_pairs={{0,1},{1,2},{2,3},{4,5},{5,6},{6,7},{8,9},{9,10},{10,11},{12,13},{... | collective-permute-start | bytes 122888 | tf_op jit(solution)/shard_map/ppermute | solution.py:29
  77.5 5.9 %collective-permute-start.12 = (f32[1,8,256]{2,1,0:T(8,128)S(1)}, f32[1,8,256]{2,1,0:T(8,128)S(1)}, u32[]{:S(2)}, u32[]{:S(2)}) collective-permute-start(f32[1,8,256]{2,1,0:T(8,128)S(1)} %get-tuple-element.370), channel_id=1, source_target_pairs={{4,0},{8,4},{12,8},{16,12},{20,16},{24,20},{28,24},{32,28},{36,32}... | collective-permute-start | bytes 24584 | tf_op jit(solution)/shard_map/ppermute | solution.py:31
  79.5 7.7 %collective-permute-start.13 = (f32[1,8,256]{2,1,0:T(8,128)S(1)}, f32[1,8,256]{2,1,0:T(8,128)S(1)}, u32[]{:S(2)}, u32[]{:S(2)}) collective-permute-start(f32[1,8,256]{2,1,0:T(8,128)S(1)} %get-tuple-element.369), channel_id=1, source_target_pairs={{0,4},{4,8},{8,12},{12,16},{16,20},{20,24},{24,28},{28,32},{32,36}... | collective-permute-start | bytes 24584 | tf_op jit(solution)/shard_map/ppermute | solution.py:29
  90.0 35.4 %all-to-all-start.1 = ((f32[128,2,256]{2,1,0:T(2,128)}), f32[128,2,256]{2,1,0:T(2,128)S(1)}, u32[]{:S(2)}, u32[]{:S(2)}) async-start(f32[128,2,256]{2,1,0:T(2,128)} %reshape.204), calls=%async_computation.1 | async-start | bytes 524288 | tf_op jit(solution)/shard_map/all_to_all | solution.py:134
where the time goes:
time: 128 us; the launch traced here: 127 us
  starting transfers between devices  74 us (58%)
  waiting for transfers between devices  37.1 us (29%)
  other arithmetic  8.42 us (7%)
  local copies, waits for them, and re-layouts  5.97 us (5%)
    ppermute x8, starting transfers between devices, extended(): lax.ppermute(head, axis, [((i + 1) % count, i) for i in range(ends)])  25 us
    all_to_all x1, waiting for transfers between devices, on_device(): lax.all_to_all(rows_both, ('sec', 'slab'), split_axis=0, concat_axis=0, t...  23.9 us
    ppermute x8, starting transfers between devices, extended(): lax.ppermute(tail, axis, [(i, (i + 1) % count) for i in range(ends)])  23.8 us
    all_to_all x1, starting transfers between devices, on_device(): lax.all_to_all(lines_both, ('sec', 'slab'), split_axis=0, concat_axis=0,...  14.2 us
    ppermute x8, waiting for transfers between devices, extended(): lax.ppermute(tail, axis, [(i, (i + 1) % count) for i in range(ends)])  13.1 us
    all_to_all x1, starting transfers between devices, on_device(): lax.all_to_all(rows_both, ('sec', 'slab'), split_axis=0, concat_axis=0, t...  11.1 us
    reduce_sum x4, other arithmetic, ionic(): jnp.sum(gate_conduct * gates * (volts[None] - gate_reversal), axis=0)  4.01 us
  transfers between devices with their start and end apart: 18, of which 4 were waited for; matrix products, arithmetic and copies ran while one was open for 9% of the time, Pallas kernels for 0%

commit v1 on v0

v1 whole, which is shorter than its diff:
```python
import functools

import jax
import jax.numpy as jnp
import numpy as np
from jax import lax
from jax.experimental import pallas as pl
from jax.experimental.pallas import tpu as pltpu
from jax.sharding import PartitionSpec as P

STEPS = 4
CAP = 2
GATES = 18
LANES = 128
SEGMENTS = 5
MESH = pl.DeviceIdType.MESH

gate_half = np.linspace(-1.5, 1.5, GATES)
gate_slope = 0.3 + 0.1 * (np.arange(GATES) % 4)
gate_decay = np.exp(-1.0 / (2.0 * 30.0 ** (np.arange(GATES) / 17.0)))
gate_conduct = 0.02 + 0.01 * (np.arange(GATES) % 3)
gate_reversal = np.linspace(-1.0, 1.0, GATES)
relax_omega = 1.5625


def iota(shape, dim):
    return lax.broadcasted_iota(jnp.int32, shape, dim)


def split_halves(x):
    high = x.astype(jnp.bfloat16)
    low = (x - high.astype(jnp.float32)).astype(jnp.bfloat16)
    return jnp.concatenate([high, low], axis=0)


def matmul(a, b, contract):
    return lax.dot_general(
        a, b, (contract, ((), ())), preferred_element_type=jnp.float32
    )


def kernel(
    n_slab, n_col,
    vol, line_hbm, dest_hbm, target_hbm, out,
    pots, coef, coef_src, faces, halo_x, halo_y,
    picks, rows_out, rows_in, lines_out, lines_in, meta,
    load_sem, meta_sem, send_sem, recv_sem, row_sem, line_sem,
):
    sec = lax.axis_index("sec")
    slab = lax.axis_index("slab")
    col = lax.axis_index("col")
    slab_low, slab_high = lax.rem(slab + n_slab - 1, n_slab), lax.rem(slab + 1, n_slab)
    col_low, col_high = lax.rem(col + n_col - 1, n_col), lax.rem(col + 1, n_col)
    nx, ny, nz = vol.shape[2], vol.shape[3], vol.shape[4]
    tx = SEGMENTS * nx
    plane = (ny, nz)
    sub, lane = iota(plane, 0), iota(plane, 1)
    low_y = jnp.logical_and(sub == 0, col > 0)
    high_y = jnp.logical_and(sub == ny - 1, col < n_col - 1)

    def load(index, src, dst):
        copy = pltpu.make_async_copy(src, dst, load_sem.at[index])
        copy.start()
        return copy

    barrier = pltpu.get_barrier_semaphore()
    neighbours = (
        (sec, slab_low, col), (sec, slab_high, col), (sec, slab, col_low), (sec, slab, col_high),
    )

    def greet():
        for there in neighbours:
            pl.semaphore_signal(barrier, inc=1, device_id=there, device_id_type=MESH)

    def exchange(step, first, last, width):
        return [
            pltpu.make_async_remote_copy(
                src_ref=src, dst_ref=dst, send_sem=send_sem.at[step, way],
                recv_sem=recv_sem.at[step, way], device_id=neighbours[way], device_id_type=MESH,
            )
            for way, (src, dst) in enumerate(
                (
                    (first, halo_x.at[step, 1]),
                    (last, halo_x.at[step, 0]),
                    (faces.at[step, 0, pl.ds(0, width)], halo_y.at[step, 1, pl.ds(0, width)]),
                    (faces.at[step, 1, pl.ds(0, width)], halo_y.at[step, 0, pl.ds(0, width)]),
                )
            )
        ]

    def to_all(src, dst, sems):
        def send(i, _):
            there = lax.rem(slab + i, n_slab)
            pltpu.make_async_remote_copy(
                src_ref=src.at[there], dst_ref=dst.at[slab], send_sem=sems.at[0],
                recv_sem=sems.at[1], device_id=(1, there, col), device_id_type=MESH,
            ).start()
            return 0

        lax.fori_loop(0, n_slab, send, 0)

    def wait_whole(ref, sem):
        pltpu.make_async_copy(ref, ref, sem).wait()

    def heart():
        loads = [
            load(0, vol.at[0, 0], pots.at[0, 0]),
            load(1, vol.at[0, pl.ds(1, GATES + 1)], out.at[0, pl.ds(1, GATES + 1)]),
        ]
        metas = [
            pltpu.make_async_copy(src.at[0], meta.at[i], meta_sem.at[i])
            for i, src in enumerate((line_hbm, dest_hbm, target_hbm))
        ]
        for copy in metas:
            copy.start()
        greet()

        for copy in metas:
            copy.wait()
        epi = meta.shape[2]
        line, dest, target = meta[0], meta[1], meta[2]
        slots = 4 * n_slab
        own = iota((slots, epi), 0)
        marks = own // 4 == dest
        before = (iota((epi, epi), 0) < iota((epi, epi), 1)).astype(jnp.bfloat16)
        rank = matmul(marks.astype(jnp.float32).astype(jnp.bfloat16), before, ((1,), (0,)))
        wanted = ((own // 2) % 2).astype(jnp.float32)
        place = jnp.logical_and(marks, rank == wanted)
        half = (own % 2).astype(jnp.float32)
        place = place.astype(jnp.float32)
        places = jnp.concatenate([place * (1.0 - half), place * half], axis=1)
        lines = nx * ny
        held = (iota((lines, epi), 0) == line).astype(jnp.float32).astype(jnp.bfloat16)
        for h in range(2):
            part = matmul(
                places[:, h * epi : (h + 1) * epi].astype(jnp.bfloat16), held, ((1,), (1,))
            ).astype(jnp.bfloat16)
            picks[:, h * lines : (h + 1) * lines] = part
            picks[:, (h + 2) * lines : (h + 3) * lines] = part
        own_d = iota((n_slab, epi), 0)
        marks_d = own_d == dest
        rank_d = matmul(marks_d.astype(jnp.float32).astype(jnp.bfloat16), before, ((1,), (0,)))
        goals = []
        for r in range(CAP):
            chosen = jnp.logical_and(marks_d, rank_d == float(r))
            goal = jnp.where(chosen, (target + 1).astype(jnp.float32), 0.0)
            goals.append(jnp.sum(goal, axis=1, keepdims=True) - 1.0)
        lane_s = iota((n_slab, LANES), 1)
        lines_out[:, 0, :] = jnp.where(lane_s < n_slab, goals[0], goals[1])

        loads[0].wait()
        for face, row in enumerate((0, ny - 1)):
            for x in range(nx):
                faces[0, face, x : x + 1, :] = pots[0, 0, x, row : row + 1, :]
        pl.semaphore_wait(barrier, 4 + n_slab)
        sends = exchange(0, pots.at[0, 0, 0], pots.at[0, 0, nx - 1], nx)
        for copy in sends:
            copy.start()
        to_all(lines_out, lines_in, line_sem)
        loads[1].wait()

        started = list(sends)
        for step in range(STEPS):

            def inner(x, _):
                volts = pots[step, 0, x]
                sigma = out[0, GATES + 1, x]
                beside_x = pots[step, 0, jnp.maximum(x - 1, 0)]
                beside_x += pots[step, 0, jnp.minimum(x + 1, nx - 1)]
                beside = jnp.where(sub == 0, volts, pltpu.roll(volts, 1, 0))
                beside += jnp.where(sub == ny - 1, volts, pltpu.roll(volts, ny - 1, 0))
                beside += jnp.where(lane == 0, volts, pltpu.roll(volts, 1, 1))
                beside += jnp.where(lane == nz - 1, volts, pltpu.roll(volts, nz - 1, 1))
                flux = 0.12 * (beside_x - 2.0 * volts) + 0.04 * (beside - 4.0 * volts)
                scaled = {}
                sums, weighted = {}, {}
                for j in range(GATES):
                    slope = float(0.5 / gate_slope[j])
                    if slope not in scaled:
                        scaled[slope] = volts * slope
                    bend = jnp.tanh(scaled[slope] - float(gate_half[j] * slope))
                    rest = float(0.5 * (1.0 - gate_decay[j]))
                    gate = out[0, 1 + j, x] * float(gate_decay[j]) + (rest * bend + rest)
                    out[0, 1 + j, x] = gate
                    conduct = float(gate_conduct[j])
                    drawn = gate * float(gate_reversal[j])
                    if conduct in sums:
                        sums[conduct] += gate
                        weighted[conduct] += drawn
                    else:
                        sums[conduct], weighted[conduct] = gate, drawn
                current = sum(c * (volts * sums[c] - weighted[c]) for c in sums)
                pots[step + 1, 0, x] = volts + sigma * flux - current
                return 0

            lax.fori_loop(0, nx, inner, 0)
            for copy in sends:
                copy.wait_recv()
            for x, here, there in ((0, slab > 0, 0), (nx - 1, slab < n_slab - 1, 1)):
                gain = jnp.where(here, 0.12, 0.0)
                pots[step + 1, 0, x] += gain * out[0, GATES + 1, x] * (
                    halo_x[step, there] - pots[step, 0, x]
                )

            for x in range(nx):
                volts = pots[step, 0, x]
                beyond = jnp.where(low_y, halo_y[step, 0, x : x + 1, :] - volts, 0.0)
                beyond += jnp.where(high_y, halo_y[step, 1, x : x + 1, :] - volts, 0.0)
                fresh = pots[step + 1, 0, x] + 0.04 * out[0, GATES + 1, x] * beyond
                pots[step + 1, 0, x] = fresh
                if step + 1 < STEPS:
                    faces[step + 1, 0, x : x + 1, :] = fresh[:1]
                    faces[step + 1, 1, x : x + 1, :] = fresh[ny - 1 :]
                else:
                    out[0, 0, x] = fresh
            if step + 1 < STEPS:
                sends = exchange(step + 1, pots.at[step + 1, 0, 0], pots.at[step + 1, 0, nx - 1], nx)
                for copy in sends:
                    copy.start()
                started += sends

        final = pots[STEPS, 0].reshape(lines, nz)
        source = jnp.concatenate([final[:, :LANES], final[:, LANES:]], axis=0)
        rows = matmul(picks[...], split_halves(source), ((1,), (0,)))
        rows_out[...] = rows.reshape(n_slab, 4, LANES)
        to_all(rows_out, rows_in, row_sem)
        for copy in started:
            copy.wait_send()
        wait_whole(lines_out, line_sem.at[0])
        wait_whole(rows_out, row_sem.at[0])

    def torso():
        def field(ref, f):
            return ref.at[0, pl.ds(SEGMENTS * f, SEGMENTS)]

        loads = [
            load(0, field(vol, 0), pots.at[0]),
            load(1, field(vol, 2), field(out, 2)),
            load(2, field(vol, 3), coef_src),
            load(3, field(vol, 1), field(out, 1)),
        ]
        greet()

        def invite(i, _):
            pl.semaphore_signal(
                barrier, inc=1, device_id=(0, lax.rem(slab + i, n_slab), col), device_id_type=MESH
            )
            return 0

        lax.fori_loop(0, n_slab, invite, 0)
        loads[0].wait()
        for face, row in enumerate((0, ny - 1)):
            for x in range(tx):
                faces[0, face, x : x + 1, :] = pots[0, x // nx, x % nx, row : row + 1, :]
        pl.semaphore_wait(barrier, 4)
        sends = exchange(0, pots.at[0, 0, 0], pots.at[0, SEGMENTS - 1, nx - 1], tx)
        for copy in sends:
            copy.start()
        for copy in loads[1:]:
            copy.wait()

        started = list(sends)
        mass = field(out, 2)
        for step in range(STEPS):
            now = pots.at[step]
            fresh_ref = pots.at[step + 1]
            before = pots.at[step - 1] if step else field(out, 1)

            def inner(k, _):
                planes = [now[k, r] for r in range(nx)]
                below = jnp.where(k > 0, now[jnp.maximum(k - 1, 0), nx - 1], 0.0)
                above = jnp.where(k < SEGMENTS - 1, now[jnp.minimum(k + 1, SEGMENTS - 1), 0], 0.0)
                around = [below] + planes + [above]
                for r in range(nx):
                    here = planes[r]
                    beside = around[r] + around[r + 2]
                    beside += jnp.where(sub == 0, 0.0, pltpu.roll(here, 1, 0))
                    beside += jnp.where(sub == ny - 1, 0.0, pltpu.roll(here, ny - 1, 0))
                    beside += jnp.where(lane == 0, 0.0, pltpu.roll(here, 1, 1))
                    beside += jnp.where(lane == nz - 1, 0.0, pltpu.roll(here, nz - 1, 1))
                    if step == 0:
                        gain = relax_omega / (6.0 + mass[k, r])
                        drive = gain * coef_src[k, r]
                        coef[k, r] = gain
                        coef_src[k, r] = drive
                    else:
                        gain = coef[k, r]
                        drive = coef_src[k, r]
                    fresh_ref[k, r] = (
                        drive + (1.0 - relax_omega) * before[k, r] + gain * beside
                    )
                return 0

            lax.fori_loop(0, SEGMENTS, inner, 0)
            for copy in sends:
                copy.wait_recv()
            for k, r, here, there in (
                (0, 0, slab > 0, 0), (SEGMENTS - 1, nx - 1, slab < n_slab - 1, 1),
            ):
                fresh_ref[k, r] += jnp.where(here, 1.0, 0.0) * coef[k, r] * halo_x[step, there]

            def outer(k, _):
                base = k * nx
                low = halo_y[step, 0, pl.ds(base, nx), :]
                high = halo_y[step, 1, pl.ds(base, nx), :]
                for r in range(nx):
                    beyond = jnp.where(low_y, low[r : r + 1], 0.0)
                    beyond += jnp.where(high_y, high[r : r + 1], 0.0)
                    fresh = fresh_ref[k, r] + coef[k, r] * beyond
                    fresh_ref[k, r] = fresh
                    if step + 1 < STEPS:
                        faces[step + 1, 0, pl.ds(base + r, 1), :] = fresh[:1]
                        faces[step + 1, 1, pl.ds(base + r, 1), :] = fresh[ny - 1 :]
                    if step + 2 == STEPS:
                        out[0, SEGMENTS + k, r] = fresh
                    if step + 1 == STEPS:
                        out[0, k, r] = fresh
                return 0

            lax.fori_loop(0, SEGMENTS, outer, 0)
            if step + 1 < STEPS:
                sends = exchange(
                    step + 1, fresh_ref.at[0, 0], fresh_ref.at[SEGMENTS - 1, nx - 1], tx
                )
                for copy in sends:
                    copy.start()
                started += sends

        wait_whole(lines_in, line_sem.at[1])
        marks = jnp.where(
            iota((n_slab, LANES), 0) == iota((n_slab, LANES), 1) % n_slab, lines_in[:, 0, :], 0.0
        )
        marks = jnp.sum(marks, axis=0, keepdims=True)[:, : CAP * n_slab]
        goals = iota((tx * ny, CAP * n_slab), 0).astype(jnp.float32)
        hits = (goals == marks).astype(jnp.float32).astype(jnp.bfloat16)
        wait_whole(rows_in, row_sem.at[1])
        got = jnp.concatenate(
            [
                jnp.concatenate([rows_in[:, 2 * r + h, :] for r in range(CAP)], axis=0)
                for h in range(2)
            ],
            axis=1,
        )
        inflow = matmul(jnp.concatenate([hits, hits], axis=1), split_halves(got), ((1,), (0,)))
        out[0, pl.ds(3 * SEGMENTS, SEGMENTS)] = inflow.reshape(SEGMENTS, nx, ny, nz)
        for copy in started:
            copy.wait_send()

    pl.when(sec == 0)(heart)
    pl.when(sec == 1)(torso)


def solution(mesh):
    n_slab, n_col = mesh.shape["slab"], mesh.shape["col"]

    def on_device(volume, epi_line, epi_dest, epi_target):
        _, fields, nx, ny, nz = volume.shape
        epi = epi_line.shape[-1]
        tx = SEGMENTS * nx
        f32 = jnp.float32
        return pl.pallas_call(
            functools.partial(kernel, n_slab, n_col),
            out_shape=jax.ShapeDtypeStruct(volume.shape, f32),
            in_specs=[pl.BlockSpec(memory_space=pl.ANY)] * 4,
            out_specs=pl.BlockSpec(memory_space=pltpu.VMEM),
            scratch_shapes=[
                pltpu.VMEM((STEPS + 1, SEGMENTS, nx, ny, nz), f32),
                pltpu.VMEM((SEGMENTS, nx, ny, nz), f32),
                pltpu.VMEM((SEGMENTS, nx, ny, nz), f32),
                pltpu.VMEM((STEPS, 2, tx, nz), f32),
                pltpu.VMEM((STEPS, 2, ny, nz), f32),
                pltpu.VMEM((STEPS, 2, tx, nz), f32),
                pltpu.VMEM((4 * n_slab, 4 * nx * ny), jnp.bfloat16),
                pltpu.VMEM((n_slab, 4, LANES), f32),
                pltpu.VMEM((n_slab, 4, LANES), f32),
                pltpu.VMEM((n_slab, 1, LANES), f32),
                pltpu.VMEM((n_slab, 1, LANES), f32),
                pltpu.VMEM((3, 1, epi), jnp.int32),
                pltpu.SemaphoreType.DMA((4,)),
                pltpu.SemaphoreType.DMA((3,)),
                pltpu.SemaphoreType.DMA((STEPS, 4)),
                pltpu.SemaphoreType.DMA((STEPS, 4)),
                pltpu.SemaphoreType.DMA((2,)),
                pltpu.SemaphoreType.DMA((2,)),
            ],
            compiler_params=pltpu.CompilerParams(
                collective_id=0, has_side_effects=True, vmem_limit_bytes=24 * 1024 * 1024
            ),
        )(volume, epi_line, epi_dest.reshape(epi_line.shape), epi_target)

    return jax.shard_map(
        on_device,
        mesh=mesh,
        in_specs=(
            P("sec", None, "slab", "col", None),
            P("slab", "col", None),
            P("slab", "col", None, None),
            P("slab", "col", None),
        ),
        out_specs=P("sec", None, "slab", "col", None),
        check_vma=False,
    )
```

time: 128 us -> 48.7 us (0.38)
  the two profiles are of different devices: /device:TPU:2 before, /device:TPU:24 now
where the time goes in v1:
time: 48.7 us; the launch traced here: 48.5 us
  Pallas kernels  44.2 us (91%)
  local copies, waits for them, and re-layouts  4.34 us (9%)
    pallas_call x1, Pallas kernels, on_device(): pl.pallas_call(functools.partial(kernel, n_slab, n_col), out_shape=jax.Sh...  44.2 us
    unnamed x9, local copies, waits for them, and re-layouts  4.34 us

profile of v1, /device:TPU:24, one launch (start us, length us, event | category | flops | bytes accessed | tf_op | source)
XLA Modules:
  0.0 48.5 jit_solution(814416380208737243)
XLA Ops:
  0.0 0.0 copy-start
  0.0 1.3 %copy-done = f32[1,20,8,8,256]{4,3,2,1,0:T(8,128)S(1)} copy-done((f32[1,20,8,8,256]{4,3,2,1,0:T(8,128)S(1)}, f32[1,20,8,8,256]{4,3,2,1,0:T(8,128)}, u32[]{:S(2)}) %copy-start) | copy-done | bytes 1310744
  1.3 0.0 copy-start.1
  1.3 0.7 %copy-done.1 = s32[1,1,64]{2,1,0:T(1,128)S(1)} copy-done((s32[1,1,64]{2,1,0:T(1,128)S(1)}, s32[1,1,64]{2,1,0:T(1,128)}, u32[]{:S(2)}) %copy-start.1) | copy-done | bytes 280
  2.0 0.0 copy-start.2
  2.0 0.7 %copy-done.2 = s32[1,1,64,1]{2,3,1,0:T(1,128)S(1)} copy-done((s32[1,1,64,1]{2,3,1,0:T(1,128)S(1)}, s32[1,1,64,1]{2,3,1,0:T(1,128)}, u32[]{:S(2)}) %copy-start.2) | copy-done | bytes 280
  2.6 0.0 copy-start.3
  2.6 0.7 %copy-done.3 = s32[1,1,64]{2,1,0:T(1,128)S(1)} copy-done((s32[1,1,64]{2,1,0:T(1,128)S(1)}, s32[1,1,64]{2,1,0:T(1,128)}, u32[]{:S(2)}) %copy-start.3) | copy-done | bytes 280
  3.3 44.2 %shard_map.46 = f32[1,20,8,8,256]{4,3,2,1,0:T(8,128)S(1)} custom-call(f32[1,20,8,8,256]{4,3,2,1,0:T(8,128)S(1)} %copy-done, s32[1,1,64]{2,1,0:T(1,128)S(1)} %copy-done.1, s32[1,1,64]{2,1,0:T(1,128)S(1)} %bitcast.1, s32[1,1,64]{2,1,0:T(1,128)S(1)} %copy-done.3), custom_call_target="tpu_custom_call" | custom-call | tf_op jit(solution)/shard_map/pallas_call | solution.py:361
  47.5 1.1 %copy.6 = f32[1,20,8,8,256]{4,3,2,1,0:T(8,128)} copy(f32[1,20,8,8,256]{4,3,2,1,0:T(8,128)S(1)} %shard_map.46) | data formatting | bytes 2621440
Async XLA Ops:
  0.0 1.3 %copy-start = (f32[1,20,8,8,256]{4,3,2,1,0:T(8,128)S(1)}, f32[1,20,8,8,256]{4,3,2,1,0:T(8,128)}, u32[]{:S(2)}) copy-start(f32[1,20,8,8,256]{4,3,2,1,0:T(8,128)} %vol.1) | copy-start | bytes 3932164
  1.3 0.7 %copy-start.1 = (s32[1,1,64]{2,1,0:T(1,128)S(1)}, s32[1,1,64]{2,1,0:T(1,128)}, u32[]{:S(2)}) copy-start(s32[1,1,64]{2,1,0:T(1,128)} %line_hbm.1) | copy-start | bytes 772
  2.0 0.7 %copy-start.2 = (s32[1,1,64,1]{2,3,1,0:T(1,128)S(1)}, s32[1,1,64,1]{2,3,1,0:T(1,128)}, u32[]{:S(2)}) copy-start(s32[1,1,64,1]{2,3,1,0:T(1,128)} %param.6) | copy-start | bytes 772
  2.6 0.7 %copy-start.3 = (s32[1,1,64]{2,1,0:T(1,128)S(1)}, s32[1,1,64]{2,1,0:T(1,128)}, u32[]{:S(2)}) copy-start(s32[1,1,64]{2,1,0:T(1,128)} %target_hbm.1) | copy-start | bytes 772

commit v2 on v1

--- a/solution.py
+++ b/solution.py
@@ -13,6 +13,7 @@
 GATES = 18
 LANES = 128
 SEGMENTS = 5
+VMEM_LIMIT = 24 * 1024 * 1024
 MESH = pl.DeviceIdType.MESH
 
 gate_half = np.linspace(-1.5, 1.5, GATES)
@@ -39,73 +40,71 @@
     )
 
 
-def kernel(
-    n_slab, n_col,
-    vol, line_hbm, dest_hbm, target_hbm, out,
-    pots, coef, coef_src, faces, halo_x, halo_y,
-    picks, rows_out, rows_in, lines_out, lines_in, meta,
-    load_sem, meta_sem, send_sem, recv_sem, row_sem, line_sem,
-):
-    sec = lax.axis_index("sec")
-    slab = lax.axis_index("slab")
-    col = lax.axis_index("col")
-    slab_low, slab_high = lax.rem(slab + n_slab - 1, n_slab), lax.rem(slab + 1, n_slab)
-    col_low, col_high = lax.rem(col + n_col - 1, n_col), lax.rem(col + 1, n_col)
-    nx, ny, nz = vol.shape[2], vol.shape[3], vol.shape[4]
-    tx = SEGMENTS * nx
-    plane = (ny, nz)
-    sub, lane = iota(plane, 0), iota(plane, 1)
-    low_y = jnp.logical_and(sub == 0, col > 0)
-    high_y = jnp.logical_and(sub == ny - 1, col < n_col - 1)
-
-    def load(index, src, dst):
-        copy = pltpu.make_async_copy(src, dst, load_sem.at[index])
-        copy.start()
-        return copy
-
-    barrier = pltpu.get_barrier_semaphore()
-    neighbours = (
-        (sec, slab_low, col), (sec, slab_high, col), (sec, slab, col_low), (sec, slab, col_high),
-    )
-
-    def greet():
-        for there in neighbours:
-            pl.semaphore_signal(barrier, inc=1, device_id=there, device_id_type=MESH)
-
-    def exchange(step, first, last, width):
+class Place:
+    def __init__(self, n_slab, n_col, sizes):
+        self.n_slab, self.n_col = n_slab, n_col
+        self.sec = sec = lax.axis_index("sec")
+        self.slab = slab = lax.axis_index("slab")
+        self.col = col = lax.axis_index("col")
+        slab_low, slab_high = lax.rem(slab + n_slab - 1, n_slab), lax.rem(slab + 1, n_slab)
+        col_low, col_high = lax.rem(col + n_col - 1, n_col), lax.rem(col + 1, n_col)
+        self.neighbours = (
+            (sec, slab_low, col), (sec, slab_high, col),
+            (sec, slab, col_low), (sec, slab, col_high),
+        )
+        _, _, _, ny, nz = sizes
+        self.sub, self.lane = iota((ny, nz), 0), iota((ny, nz), 1)
+        self.low_y = jnp.logical_and(self.sub == 0, col > 0)
+        self.high_y = jnp.logical_and(self.sub == ny - 1, col < n_col - 1)
+
+    def greet(self):
+        for there in self.neighbours:
+            pl.semaphore_signal(
+                pltpu.get_barrier_semaphore(), inc=1, device_id=there, device_id_type=MESH
+            )
+
+    def exchange(self, step, first, last, faces, halo_x, halo_y, send_sem, recv_sem):
+        pairs = (
+            (first, halo_x.at[step, 1]),
+            (last, halo_x.at[step, 0]),
+            (faces.at[step, 0], halo_y.at[step, 1]),
+            (faces.at[step, 1], halo_y.at[step, 0]),
+        )
         return [
             pltpu.make_async_remote_copy(
                 src_ref=src, dst_ref=dst, send_sem=send_sem.at[step, way],
-                recv_sem=recv_sem.at[step, way], device_id=neighbours[way], device_id_type=MESH,
+                recv_sem=recv_sem.at[step, way], device_id=self.neighbours[way],
+                device_id_type=MESH,
             )
-            for way, (src, dst) in enumerate(
-                (
-                    (first, halo_x.at[step, 1]),
-                    (last, halo_x.at[step, 0]),
-                    (faces.at[step, 0, pl.ds(0, width)], halo_y.at[step, 1, pl.ds(0, width)]),
-                    (faces.at[step, 1, pl.ds(0, width)], halo_y.at[step, 0, pl.ds(0, width)]),
-                )
-            )
+            for way, (src, dst) in enumerate(pairs)
         ]
 
-    def to_all(src, dst, sems):
-        def send(i, _):
-            there = lax.rem(slab + i, n_slab)
-            pltpu.make_async_remote_copy(
-                src_ref=src.at[there], dst_ref=dst.at[slab], send_sem=sems.at[0],
-                recv_sem=sems.at[1], device_id=(1, there, col), device_id_type=MESH,
-            ).start()
-            return 0
-
-        lax.fori_loop(0, n_slab, send, 0)
-
-    def wait_whole(ref, sem):
-        pltpu.make_async_copy(ref, ref, sem).wait()
+
+def load(src, dst, sem):
+    copy = pltpu.make_async_copy(src, dst, sem)
+    copy.start()
+    return copy
+
+
+def wait_whole(ref, sem):
+    pltpu.make_async_copy(ref, ref, sem).wait()
+
+
+def heart_kernel(
+    n_slab, n_col,
+    vol, line_hbm, dest_hbm, target_hbm, state, rows_out,
+    pots, faces, halo_x, halo_y, picks, meta,
+    load_sem, meta_sem, send_sem, recv_sem,
+):
+    place_ = Place(n_slab, n_col, vol.shape)
+    slab, sub, lane = place_.slab, place_.sub, place_.lane
+    low_y, high_y = place_.low_y, place_.high_y
+    nx, ny, nz = vol.shape[2:]
 
     def heart():
         loads = [
-            load(0, vol.at[0, 0], pots.at[0, 0]),
-            load(1, vol.at[0, pl.ds(1, GATES + 1)], out.at[0, pl.ds(1, GATES + 1)]),
+            load(vol.at[0, 0], pots.at[0], load_sem.at[0]),
+            load(vol.at[0, pl.ds(1, GATES + 1)], state.at[pl.ds(1, GATES + 1)], load_sem.at[1]),
         ]
         metas = [
             pltpu.make_async_copy(src.at[0], meta.at[i], meta_sem.at[i])
@@ -113,7 +112,7 @@
         ]
         for copy in metas:
             copy.start()
-        greet()
+        place_.greet()
 
         for copy in metas:
             copy.wait()
@@ -146,27 +145,27 @@
             goal = jnp.where(chosen, (target + 1).astype(jnp.float32), 0.0)
             goals.append(jnp.sum(goal, axis=1, keepdims=True) - 1.0)
         lane_s = iota((n_slab, LANES), 1)
-        lines_out[:, 0, :] = jnp.where(lane_s < n_slab, goals[0], goals[1])
+        rows_out[:, 4, :] = jnp.where(lane_s < n_slab, goals[0], goals[1])
 
         loads[0].wait()
         for face, row in enumerate((0, ny - 1)):
             for x in range(nx):
-                faces[0, face, x : x + 1, :] = pots[0, 0, x, row : row + 1, :]
-        pl.semaphore_wait(barrier, 4 + n_slab)
-        sends = exchange(0, pots.at[0, 0, 0], pots.at[0, 0, nx - 1], nx)
+                faces[0, face, x : x + 1, :] = pots[0, x, row : row + 1, :]
+        pl.semaphore_wait(pltpu.get_barrier_semaphore(), 4)
+        links = (faces, halo_x, halo_y, send_sem, recv_sem)
+        sends = place_.exchange(0, pots.at[0, 0], pots.at[0, nx - 1], *links)
         for copy in sends:
             copy.start()
-        to_all(lines_out, lines_in, line_sem)
         loads[1].wait()
 
         started = list(sends)
         for step in range(STEPS):
 
             def inner(x, _):
-                volts = pots[step, 0, x]
-                sigma = out[0, GATES + 1, x]
-                beside_x = pots[step, 0, jnp.maximum(x - 1, 0)]
-                beside_x += pots[step, 0, jnp.minimum(x + 1, nx - 1)]
+                volts = pots[step, x]
+                sigma = state[GATES + 1, x]
+                beside_x = pots[step, jnp.maximum(x - 1, 0)]
+                beside_x += pots[step, jnp.minimum(x + 1, nx - 1)]
                 beside = jnp.where(sub == 0, volts, pltpu.roll(volts, 1, 0))
                 beside += jnp.where(sub == ny - 1, volts, pltpu.roll(volts, ny - 1, 0))
                 beside += jnp.where(lane == 0, volts, pltpu.roll(volts, 1, 1))
@@ -180,8 +179,8 @@
                         scaled[slope] = volts * slope
                     bend = jnp.tanh(scaled[slope] - float(gate_half[j] * slope))
                     rest = float(0.5 * (1.0 - gate_decay[j]))
-                    gate = out[0, 1 + j, x] * float(gate_decay[j]) + (rest * bend + rest)
-                    out[0, 1 + j, x] = gate
+                    gate = state[1 + j, x] * float(gate_decay[j]) + (rest * bend + rest)
+                    state[1 + j, x] = gate
                     conduct = float(gate_conduct[j])
                     drawn = gate * float(gate_reversal[j])
                     if conduct in sums:
@@ -190,7 +189,7 @@
                     else:
                         sums[conduct], weighted[conduct] = gate, drawn
                 current = sum(c * (volts * sums[c] - weighted[c]) for c in sums)
-                pots[step + 1, 0, x] = volts + sigma * flux - current
+                pots[step + 1, x] = volts + sigma * flux - current
                 return 0
 
             lax.fori_loop(0, nx, inner, 0)
@@ -198,35 +197,64 @@
                 copy.wait_recv()
             for x, here, there in ((0, slab > 0, 0), (nx - 1, slab < n_slab - 1, 1)):
                 gain = jnp.where(here, 0.12, 0.0)
-                pots[step + 1, 0, x] += gain * out[0, GATES + 1, x] * (
-                    halo_x[step, there] - pots[step, 0, x]
+                pots[step + 1, x] += gain * state[GATES + 1, x] * (
+                    halo_x[step, there] - pots[step, x]
                 )
 
             for x in range(nx):
-                volts = pots[step, 0, x]
+                volts = pots[step, x]
                 beyond = jnp.where(low_y, halo_y[step, 0, x : x + 1, :] - volts, 0.0)
                 beyond += jnp.where(high_y, halo_y[step, 1, x : x + 1, :] - volts, 0.0)
-                fresh = pots[step + 1, 0, x] + 0.04 * out[0, GATES + 1, x] * beyond
-                pots[step + 1, 0, x] = fresh
+                fresh = pots[step + 1, x] + 0.04 * state[GATES + 1, x] * beyond
+                pots[step + 1, x] = fresh
                 if step + 1 < STEPS:
                     faces[step + 1, 0, x : x + 1, :] = fresh[:1]
                     faces[step + 1, 1, x : x + 1, :] = fresh[ny - 1 :]
                 else:
-                    out[0, 0, x] = fresh
+                    state[0, x] = fresh
             if step + 1 < STEPS:
-                sends = exchange(step + 1, pots.at[step + 1, 0, 0], pots.at[step + 1, 0, nx - 1], nx)
+                sends = place_.exchange(step + 1, pots.at[step + 1, 0], pots.at[step + 1, nx - 1], *links)
                 for copy in sends:
                     copy.start()
                 started += sends
 
-        final = pots[STEPS, 0].reshape(lines, nz)
+        final = pots[STEPS].reshape(lines, nz)
         source = jnp.concatenate([final[:, :LANES], final[:, LANES:]], axis=0)
         rows = matmul(picks[...], split_halves(source), ((1,), (0,)))
-        rows_out[...] = rows.reshape(n_slab, 4, LANES)
-        to_all(rows_out, rows_in, row_sem)
+        rows_out[:, :4, :] = rows.reshape(n_slab, 4, LANES)
         for copy in started:
             copy.wait_send()
-        wait_whole(lines_out, line_sem.at[0])
+
+    pl.when(place_.sec == 0)(heart)
+
+
+def torso_kernel(
+    n_slab, n_col,
+    vol, state, rows_out, out,
+    pots, coef, coef_src, faces, halo_x, halo_y, rows_in,
+    load_sem, send_sem, recv_sem, row_sem,
+):
+    place_ = Place(n_slab, n_col, vol.shape)
+    slab, col, sub, lane = place_.slab, place_.col, place_.sub, place_.lane
+    low_y, high_y = place_.low_y, place_.high_y
+    nx, ny, nz = vol.shape[2:]
+    tx = SEGMENTS * nx
+    barrier = pltpu.get_barrier_semaphore()
+
+    def heart():
+        keep = load(state, out.at[0], load_sem.at[0])
+        pl.semaphore_wait(barrier, n_slab)
+
+        def send(i, _):
+            there = lax.rem(slab + i, n_slab)
+            pltpu.make_async_remote_copy(
+                src_ref=rows_out.at[there], dst_ref=rows_in.at[slab], send_sem=row_sem.at[0],
+                recv_sem=row_sem.at[1], device_id=(1, there, col), device_id_type=MESH,
+            ).start()
+            return 0
+
+        lax.fori_loop(0, n_slab, send, 0)
+        keep.wait()
         wait_whole(rows_out, row_sem.at[0])
 
     def torso():
@@ -234,12 +262,12 @@
             return ref.at[0, pl.ds(SEGMENTS * f, SEGMENTS)]
 
         loads = [
-            load(0, field(vol, 0), pots.at[0]),
-            load(1, field(vol, 2), field(out, 2)),
-            load(2, field(vol, 3), coef_src),
-            load(3, field(vol, 1), field(out, 1)),
+            load(field(vol, 0), pots.at[0], load_sem.at[0]),
+            load(field(vol, 2), field(out, 2), load_sem.at[1]),
+            load(field(vol, 3), coef_src, load_sem.at[2]),
+            load(field(vol, 1), field(out, 1), load_sem.at[3]),
         ]
-        greet()
+        place_.greet()
 
         def invite(i, _):
             pl.semaphore_signal(
@@ -253,7 +281,8 @@
             for x in range(tx):
                 faces[0, face, x : x + 1, :] = pots[0, x // nx, x % nx, row : row + 1, :]
         pl.semaphore_wait(barrier, 4)
-        sends = exchange(0, pots.at[0, 0, 0], pots.at[0, SEGMENTS - 1, nx - 1], tx)
+        links = (faces, halo_x, halo_y, send_sem, recv_sem)
+        sends = place_.exchange(0, pots.at[0, 0, 0], pots.at[0, SEGMENTS - 1, nx - 1], *links)
         for copy in sends:
             copy.start()
         for copy in loads[1:]:
@@ -319,21 +348,20 @@
 
             lax.fori_loop(0, SEGMENTS, outer, 0)
             if step + 1 < STEPS:
-                sends = exchange(
-                    step + 1, fresh_ref.at[0, 0], fresh_ref.at[SEGMENTS - 1, nx - 1], tx
+                sends = place_.exchange(
+                    step + 1, fresh_ref.at[0, 0], fresh_ref.at[SEGMENTS - 1, nx - 1], *links
                 )
                 for copy in sends:
                     copy.start()
                 started += sends
 
-        wait_whole(lines_in, line_sem.at[1])
+        wait_whole(rows_in, row_sem.at[1])
         marks = jnp.where(
-            iota((n_slab, LANES), 0) == iota((n_slab, LANES), 1) % n_slab, lines_in[:, 0, :], 0.0
+            iota((n_slab, LANES), 0) == iota((n_slab, LANES), 1) % n_slab, rows_in[:, 4, :], 0.0
         )
         marks = jnp.sum(marks, axis=0, keepdims=True)[:, : CAP * n_slab]
         goals = iota((tx * ny, CAP * n_slab), 0).astype(jnp.float32)
         hits = (goals == marks).astype(jnp.float32).astype(jnp.bfloat16)
-        wait_whole(rows_in, row_sem.at[1])
         got = jnp.concatenate(
             [
                 jnp.concatenate([rows_in[:, 2 * r + h, :] for r in range(CAP)], axis=0)
@@ -346,8 +374,8 @@
         for copy in started:
             copy.wait_send()
 
-    pl.when(sec == 0)(heart)
-    pl.when(sec == 1)(torso)
+    pl.when(place_.sec == 0)(heart)
+    pl.when(place_.sec == 1)(torso)
 
 
 def solution(mesh):
@@ -357,12 +385,37 @@
         _, fields, nx, ny, nz = volume.shape
         epi = epi_line.shape[-1]
         tx = SEGMENTS * nx
-        f32 = jnp.float32
+        f32, dma = jnp.float32, pltpu.SemaphoreType.DMA
+        fields_type = jax.ShapeDtypeStruct((fields, nx, ny, nz), f32)
+        volume, epi_line, epi_dest, epi_target = (
+            pltpu.with_memory_space_constraint(x, pltpu.HBM)
+            for x in (volume, epi_line, epi_dest.reshape(epi_line.shape), epi_target)
+        )
+        hbm = pl.BlockSpec(memory_space=pltpu.HBM)
+        vmem = pl.BlockSpec(memory_space=pltpu.VMEM)
+        state, rows = pl.pallas_call(
+            functools.partial(heart_kernel, n_slab, n_col),
+            out_shape=(fields_type, jax.ShapeDtypeStruct((n_slab, 5, LANES), f32)),
+            in_specs=[hbm] * 4,
+            out_specs=(vmem, vmem),
+            scratch_shapes=[
+                pltpu.VMEM((STEPS + 1, nx, ny, nz), f32),
+                pltpu.VMEM((STEPS, 2, nx, nz), f32),
+                pltpu.VMEM((STEPS, 2, ny, nz), f32),
+                pltpu.VMEM((STEPS, 2, nx, nz), f32),
+                pltpu.VMEM((4 * n_slab, 4 * nx * ny), jnp.bfloat16),
+                pltpu.VMEM((3, 1, epi), jnp.int32),
+                dma((2,)), dma((3,)), dma((STEPS, 4)), dma((STEPS, 4)),
+            ],
+            compiler_params=pltpu.CompilerParams(
+                collective_id=0, has_side_effects=True, vmem_limit_bytes=VMEM_LIMIT
+            ),
+        )(volume, epi_line, epi_dest, epi_target)
         return pl.pallas_call(
-            functools.partial(kernel, n_slab, n_col),
+            functools.partial(torso_kernel, n_slab, n_col),
             out_shape=jax.ShapeDtypeStruct(volume.shape, f32),
-            in_specs=[pl.BlockSpec(memory_space=pl.ANY)] * 4,
-            out_specs=pl.BlockSpec(memory_space=pltpu.VMEM),
+            in_specs=[hbm, vmem, vmem],
+            out_specs=vmem,
             scratch_shapes=[
                 pltpu.VMEM((STEPS + 1, SEGMENTS, nx, ny, nz), f32),
                 pltpu.VMEM((SEGMENTS, nx, ny, nz), f32),
@@ -370,23 +423,13 @@
                 pltpu.VMEM((STEPS, 2, tx, nz), f32),
                 pltpu.VMEM((STEPS, 2, ny, nz), f32),
                 pltpu.VMEM((STEPS, 2, tx, nz), f32),
-                pltpu.VMEM((4 * n_slab, 4 * nx * ny), jnp.bfloat16),
-                pltpu.VMEM((n_slab, 4, LANES), f32),
-                pltpu.VMEM((n_slab, 4, LANES), f32),
-                pltpu.VMEM((n_slab, 1, LANES), f32),
-                pltpu.VMEM((n_slab, 1, LANES), f32),
-                pltpu.VMEM((3, 1, epi), jnp.int32),
-                pltpu.SemaphoreType.DMA((4,)),
-                pltpu.SemaphoreType.DMA((3,)),
-                pltpu.SemaphoreType.DMA((STEPS, 4)),
-                pltpu.SemaphoreType.DMA((STEPS, 4)),
-                pltpu.SemaphoreType.DMA((2,)),
-                pltpu.SemaphoreType.DMA((2,)),
+                pltpu.VMEM((n_slab, 5, LANES), f32),
+                dma((4,)), dma((STEPS, 4)), dma((STEPS, 4)), dma((2,)),
             ],
             compiler_params=pltpu.CompilerParams(
-                collective_id=0, has_side_effects=True, vmem_limit_bytes=24 * 1024 * 1024
+                collective_id=1, has_side_effects=True, vmem_limit_bytes=VMEM_LIMIT
             ),
-        )(volume, epi_line, epi_dest.reshape(epi_line.shape), epi_target)
+        )(volume, state, rows)
 
     return jax.shard_map(
         on_device,

time: 48.7 us -> 39.1 us (0.80)
  Pallas kernels: 44.2 us -> 37.8 us
  local copies, waits for them, and re-layouts: 4.34 us -> 1.06 us
    pallas_call x1 -> x2, Pallas kernels: 44.2 us -> 37.8 us  [the longest x1 36.8 us: on_device(): pl.pallas_call(functools.partial(torso_kernel, n_slab, n_col), out_shape=...]
    unnamed x9 -> x1, local copies, waits for them, and re-layouts: 4.34 us -> 1.06 us
where the time goes in v2:
time: 39.1 us; the launch traced here: 38.9 us
  Pallas kernels  37.8 us (97%)
  local copies, waits for them, and re-layouts  1.06 us (3%)
    pallas_call x1, Pallas kernels, on_device(): pl.pallas_call(functools.partial(torso_kernel, n_slab, n_col), out_shape=...  36.8 us
    unnamed x1, local copies, waits for them, and re-layouts  1.06 us
    pallas_call x1, Pallas kernels, on_device(): pl.pallas_call(functools.partial(heart_kernel, n_slab, n_col), out_shape=...  1.04 us

profile of v2, /device:TPU:24, one launch (start us, length us, event | category | flops | bytes accessed | tf_op | source)
XLA Modules:
  0.0 38.9 jit_solution(68623974521071275)
XLA Ops:
  0.0 1.0 %shard_map.46 = (f32[20,8,8,256]{3,2,1,0:T(8,128)S(1)}, f32[64,5,128]{2,1,0:T(8,128)S(1)}) custom-call(f32[1,20,8,8,256]{4,3,2,1,0:T(8,128)} %vol.3, s32[1,1,64]{2,1,0:T(1,128)} %line_hbm.1, s32[1,1,64]{2,1,0:T(1,128)} %bitcast.1, s32[1,1,64]{2,1,0:T(1,128)} %target_hbm.1), custom_call_target="tpu_custom_call" | custom-call | tf_op jit(solution)/shard_map/pallas_call | solution.py:396
  1.0 36.8 %shard_map.47 = f32[1,20,8,8,256]{4,3,2,1,0:T(8,128)S(1)} custom-call(f32[1,20,8,8,256]{4,3,2,1,0:T(8,128)} %vol.3, f32[20,8,8,256]{3,2,1,0:T(8,128)S(1)} %get-tuple-element.7.state, f32[64,5,128]{2,1,0:T(8,128)S(1)} %get-tuple-element.8.rows_out), custom_call_target="tpu_custom_call" | custom-call | tf_op jit(solution)/shard_map/pallas_call | solution.py:414
  37.9 1.1 %copy.6 = f32[1,20,8,8,256]{4,3,2,1,0:T(8,128)} copy(f32[1,20,8,8,256]{4,3,2,1,0:T(8,128)S(1)} %shard_map.47) | data formatting | bytes 2621440

commit v3 on v2

v3 whole, which is shorter than its diff:
```python
import functools

import jax
import jax.numpy as jnp
import numpy as np
from jax import lax
from jax.experimental import pallas as pl
from jax.experimental.pallas import tpu as pltpu
from jax.sharding import PartitionSpec as P

STEPS = 4
CAP = 2
GATES = 18
LANES = 128
SEGMENTS = 5
WIDE = 2
PHASES = STEPS // WIDE
VMEM_LIMIT = 24 * 1024 * 1024
MESH = pl.DeviceIdType.MESH

gate_half = np.linspace(-1.5, 1.5, GATES)
gate_slope = 0.3 + 0.1 * (np.arange(GATES) % 4)
gate_decay = np.exp(-1.0 / (2.0 * 30.0 ** (np.arange(GATES) / 17.0)))
gate_conduct = 0.02 + 0.01 * (np.arange(GATES) % 3)
gate_reversal = np.linspace(-1.0, 1.0, GATES)
relax_omega = 1.5625


def iota(shape, dim):
    return lax.broadcasted_iota(jnp.int32, shape, dim)


def split_halves(x):
    high = x.astype(jnp.bfloat16)
    low = (x - high.astype(jnp.float32)).astype(jnp.bfloat16)
    return jnp.concatenate([high, low], axis=0)


def matmul(a, b, contract):
    return lax.dot_general(
        a, b, (contract, ((), ())), preferred_element_type=jnp.float32
    )


class Place:
    def __init__(self, n_slab, n_col, sizes):
        self.n_slab, self.n_col = n_slab, n_col
        self.sec = sec = lax.axis_index("sec")
        self.slab = slab = lax.axis_index("slab")
        self.col = col = lax.axis_index("col")
        _, _, nx, self.ny, self.nz = sizes
        plane = (self.ny, self.nz)
        self.sub, self.lane = iota(plane, 0), iota(plane, 1)
        self.exists = exists = ((slab > 0, slab < n_slab - 1), (col > 0, col < n_col - 1))
        self.low_y = jnp.logical_and(self.sub == 0, exists[1][0])
        self.high_y = jnp.logical_and(self.sub == self.ny - 1, exists[1][1])
        moves = [(i, j) for i in range(2) for j in range(2)]
        self.met = [
            (jnp.logical_and(exists[0][i], exists[1][j]), (sec, slab + 2 * i - 1, col + 2 * j - 1))
            for i, j in moves
        ]
        self.met += [(exists[0][i], (sec, slab + 2 * i - 1, col)) for i in range(2)]
        self.met += [(exists[1][j], (sec, slab, col + 2 * j - 1)) for j in range(2)]

    def greet(self):
        for here, there in self.met:

            @pl.when(here)
            def _(there=there):
                pl.semaphore_signal(
                    pltpu.get_barrier_semaphore(), inc=1, device_id=there, device_id_type=MESH
                )

    def await_met(self):
        count = sum(here.astype(jnp.int32) for here, _ in self.met)
        pl.semaphore_wait(pltpu.get_barrier_semaphore(), count)

    def exchange(self, phase, parts, send_sem, recv_sem):
        copies = []
        for way, (direction, src, dst) in parts:
            here, there = self.met[direction]
            copy = pltpu.make_async_remote_copy(
                src_ref=src, dst_ref=dst, send_sem=send_sem.at[phase, way],
                recv_sem=recv_sem.at[phase, way], device_id=there, device_id_type=MESH,
            )
            copies.append((here, copy, self.met[(3, 2, 1, 0, 5, 4, 7, 6)[direction]][0]))
        return copies

    def edges(self, phase, out_x, out_y, in_x, in_y, first, count):
        fields = pl.ds(first, count)
        return [
            (4 + 2 * axis + side, out.at[phase, side, fields], into.at[phase, 1 - side, fields])
            for axis, (out, into) in enumerate(((out_x, in_x), (out_y, in_y)))
            for side in range(2)
        ]

    def corners(self, phase, out_c, in_c):
        return [(c, out_c.at[phase, c], in_c.at[phase, 3 - c]) for c in range(4)]

    def beside_lines(self, cells, low, high):
        last = self.ny - 1
        below = jnp.where(self.sub == 0, low, pltpu.roll(cells, 1, 0))
        return below + jnp.where(self.sub == last, high, pltpu.roll(cells, last, 0))

    def beside_z(self, cells, low, high):
        last = self.nz - 1
        below = jnp.where(self.lane == 0, low, pltpu.roll(cells, 1, 1))
        return below + jnp.where(self.lane == last, high, pltpu.roll(cells, last, 1))


def start(copies):
    for here, copy, _ in copies:
        pl.when(here)(copy.start)


def wait_recv(copies):
    for _, copy, here in copies:
        pl.when(here)(copy.wait_recv)


def wait_send(copies):
    for here, copy, _ in copies:
        pl.when(here)(copy.wait_send)


def load(src, dst, sem):
    copy = pltpu.make_async_copy(src, dst, sem)
    copy.start()
    return copy


def wait_whole(ref, sem):
    pltpu.make_async_copy(ref, ref, sem).wait()


def heart_kernel(
    n_slab, n_col,
    vol, line_hbm, dest_hbm, target_hbm, state, rows_out,
    pots, moments, out_x, out_y, out_c, in_x, in_y, in_c, ring, picks, meta,
    load_sem, meta_sem, send_sem, recv_sem,
):
    place_ = Place(n_slab, n_col, vol.shape)
    low_y, high_y = place_.low_y, place_.high_y
    nx, ny, nz = vol.shape[2:]
    ends_x, ends_y = (0, nx - 1), (0, ny - 1)

    def bends(volts):
        scaled = {}
        for j in range(GATES):
            slope = float(0.5 / gate_slope[j])
            if slope not in scaled:
                scaled[slope] = volts * slope
            yield j, jnp.tanh(scaled[slope] - float(gate_half[j] * slope))

    def step_plane(step, x, with_moments):
        volts = pots[step, x]
        sigma = state[GATES + 1, x]
        beside_x = pots[step, jnp.maximum(x - 1, 0)] + pots[step, jnp.minimum(x + 1, nx - 1)]
        around = place_.beside_lines(volts, volts, volts)
        around += place_.beside_z(volts, volts, volts)
        flux = 0.12 * (beside_x - 2.0 * volts) + 0.04 * (around - 4.0 * volts)
        sums, weighted = {}, {}
        later, later_weighted = 0.0, 0.0
        for j, bend in bends(volts):
            rest = float(0.5 * (1.0 - gate_decay[j]))
            gate = state[1 + j, x] * float(gate_decay[j]) + (rest * bend + rest)
            state[1 + j, x] = gate
            conduct = float(gate_conduct[j])
            drawn = gate * float(gate_reversal[j])
            if conduct in sums:
                sums[conduct] += gate
                weighted[conduct] += drawn
            else:
                sums[conduct], weighted[conduct] = gate, drawn
            if with_moments:
                later += gate * float(gate_conduct[j] * gate_decay[j])
                later_weighted += drawn * float(gate_conduct[j] * gate_decay[j])
        if with_moments:
            moments[0, x] = later
            moments[1, x] = later_weighted
        current = sum(c * (volts * sums[c] - weighted[c]) for c in sums)
        pots[step + 1, x] = volts + sigma * flux - current

    def first_moments(x, _):
        later, later_weighted = 0.0, 0.0
        for j in range(GATES):
            part = state[1 + j, x] * float(gate_conduct[j] * gate_decay[j])
            later += part
            later_weighted += part * float(gate_reversal[j])
        moments[0, x] = later
        moments[1, x] = later_weighted
        return 0

    def send_edges(phase):
        step = WIDE * phase
        for side in range(2):
            out_x[phase, side, 0] = pots[step, ends_x[side]]
            for x in range(nx):
                y = ends_y[side]
                out_y[phase, side, 0, x : x + 1, :] = pots[step, x, y : y + 1, :]
        parts = place_.edges(phase, out_x, out_y, in_x, in_y, 0, 1)
        copies = place_.exchange(phase, list(enumerate(parts)), send_sem, recv_sem)
        start(copies)
        return copies

    def send_rest(phase):
        step = WIDE * phase
        for side in range(2):
            x = ends_x[side]
            out_x[phase, side, 1] = pots[step, x + 1 - 2 * side]
            out_x[phase, side, 2] = moments[0, x]
            out_x[phase, side, 3] = moments[1, x]
            if phase == 0:
                out_x[phase, side, 4] = state[GATES + 1, x]
            for j, y in enumerate(ends_y):
                out_c[phase, 2 * side + j] = pots[step, x, y : y + 1, :]
        for x in range(nx):
            for side, y in enumerate(ends_y):
                inward = y + 1 - 2 * side
                rows = [pots[step, x, inward : inward + 1, :]]
                rows += [moments[f, x, y : y + 1, :] for f in range(2)]
                if phase == 0:
                    rows.append(state[GATES + 1, x, y : y + 1, :])
                for f, row in enumerate(rows):
                    out_y[phase, side, 1 + f, x : x + 1, :] = row
        parts = place_.edges(phase, out_x, out_y, in_x, in_y, 1, 4 if phase == 0 else 3)
        parts += place_.corners(phase, out_c, in_c)
        copies = place_.exchange(phase, list(enumerate(parts, 4)), send_sem, recv_sem)
        start(copies)
        return copies

    def correct(step, planes, rows):
        for side, x in enumerate(ends_x):
            beyond = jnp.where(place_.exists[0][side], planes[side][...] - pots[step, x], 0.0)
            pots[step + 1, x] += 0.12 * state[GATES + 1, x] * beyond
        for x in range(nx):
            volts = pots[step, x]
            beyond = jnp.where(low_y, rows[0][x : x + 1, :] - volts, 0.0)
            beyond += jnp.where(high_y, rows[1][x : x + 1, :] - volts, 0.0)
            pots[step + 1, x] += 0.04 * state[GATES + 1, x] * beyond

    def step_ring(phase):
        step = WIDE * phase
        for axis, (into, across, along) in enumerate(((in_x, 0.12, 0.04), (in_y, 0.04, 0.12))):
            for side in range(2):
                volts, far = into[phase, side, 0], into[phase, side, 1]
                near = pots[step, ends_x[side]] if axis == 0 else out_y[phase, side, 0]
                tips = []
                for end in range(2):
                    corner = in_c[phase, 2 * side + end if axis == 0 else 2 * end + side]
                    own = volts[ends_y[end] : ends_y[end] + 1]
                    tips.append(jnp.where(place_.exists[1 - axis][end], corner, own))
                flux = across * (near + far - 2.0 * volts)
                flux += along * (place_.beside_lines(volts, *tips) - 2.0 * volts)
                flux += 0.04 * (place_.beside_z(volts, volts, volts) - 2.0 * volts)
                gain = np.float64(0.5) * gate_conduct * (1.0 - gate_decay)
                drawn, weighted = 0.0, 0.0
                for j, bend in bends(volts):
                    drawn += bend * float(gain[j])
                    weighted += bend * float(gain[j] * gate_reversal[j])
                drawn += into[phase, side, 2] + float(gain.sum())
                weighted += into[phase, side, 3] + float((gain * gate_reversal).sum())
                fresh = volts + in_sigma(axis, side) * flux - (volts * drawn - weighted)
                ring[phase, 2 * axis + side] = fresh

    def in_sigma(axis, side):
        return (in_x, in_y)[axis][0, side, 4]

    def heart():
        loads = [
            load(vol.at[0, 0], pots.at[0], load_sem.at[0]),
            load(vol.at[0, pl.ds(1, GATES + 1)], state.at[pl.ds(1, GATES + 1)], load_sem.at[1]),
        ]
        metas = [
            load(src.at[0], meta.at[i], meta_sem.at[i])
            for i, src in enumerate((line_hbm, dest_hbm, target_hbm))
        ]
        place_.greet()
        loads[0].wait()
        place_.await_met()
        edges = send_edges(0)
        loads[1].wait()
        lax.fori_loop(0, nx, first_moments, 0, unroll=2)
        rest = send_rest(0)
        started = edges + rest

        for copy in metas:
            copy.wait()
        lines = nx * ny
        fill_picks(lines)
        for phase in range(PHASES):
            step = WIDE * phase

            def first(x, _):
                step_plane(step, x, False)
                return 0

            def second(x, _):
                step_plane(step + 1, x, phase + 1 < PHASES)
                return 0

            lax.fori_loop(0, nx, first, 0, unroll=2)
            wait_recv(edges)
            correct(
                step, [in_x.at[phase, side, 0] for side in range(2)],
                [in_y.at[phase, side, 0] for side in range(2)],
            )
            lax.fori_loop(0, nx, second, 0, unroll=2)
            wait_recv(rest)
            step_ring(phase)
            correct(
                step + 1, [ring.at[phase, side] for side in range(2)],
                [ring.at[phase, 2 + side] for side in range(2)],
            )
            if phase + 1 < PHASES:
                edges = send_edges(phase + 1)
                rest = send_rest(phase + 1)
                started += edges + rest

        state[0] = pots[STEPS]
        final = pots[STEPS].reshape(lines, nz)
        source = jnp.concatenate([final[:, :LANES], final[:, LANES:]], axis=0)
        rows = matmul(picks[...], split_halves(source), ((1,), (0,)))
        rows_out[:, :4, :] = rows.reshape(n_slab, 4, LANES)
        wait_send(started)

    def fill_picks(lines):
        epi = meta.shape[2]
        line, dest, target = meta[0], meta[1], meta[2]
        slots = 4 * n_slab
        own = iota((slots, epi), 0)
        marks = own // 4 == dest
        before = (iota((epi, epi), 0) < iota((epi, epi), 1)).astype(jnp.bfloat16)
        rank = matmul(marks.astype(jnp.float32).astype(jnp.bfloat16), before, ((1,), (0,)))
        wanted = ((own // 2) % 2).astype(jnp.float32)
        place = jnp.logical_and(marks, rank == wanted)
        half = (own % 2).astype(jnp.float32)
        place = place.astype(jnp.float32)
        places = jnp.concatenate([place * (1.0 - half), place * half], axis=1)
        held = (iota((lines, epi), 0) == line).astype(jnp.float32).astype(jnp.bfloat16)
        for h in range(2):
            part = matmul(
                places[:, h * epi : (h + 1) * epi].astype(jnp.bfloat16), held, ((1,), (1,))
            ).astype(jnp.bfloat16)
            picks[:, h * lines : (h + 1) * lines] = part
            picks[:, (h + 2) * lines : (h + 3) * lines] = part
        own_d = iota((n_slab, epi), 0)
        marks_d = own_d == dest
        rank_d = matmul(marks_d.astype(jnp.float32).astype(jnp.bfloat16), before, ((1,), (0,)))
        goals = []
        for r in range(CAP):
            chosen = jnp.logical_and(marks_d, rank_d == float(r))
            goal = jnp.where(chosen, (target + 1).astype(jnp.float32), 0.0)
            goals.append(jnp.sum(goal, axis=1, keepdims=True) - 1.0)
        lane_s = iota((n_slab, LANES), 1)
        rows_out[:, 4, :] = jnp.where(lane_s < n_slab, goals[0], goals[1])

    pl.when(place_.sec == 0)(heart)


def torso_kernel(
    n_slab, n_col,
    vol, rows_out, out, rows_in,
    pots, coef, drive, out_x, out_y, out_c, in_x, in_y, in_c, ring_x, ring_y,
    load_sem, send_sem, recv_sem, row_sem,
):
    place_ = Place(n_slab, n_col, vol.shape)
    slab, col = place_.slab, place_.col
    low_y, high_y = place_.low_y, place_.high_y
    nx, ny, nz = vol.shape[2:]
    tx = SEGMENTS * nx
    barrier = pltpu.get_barrier_semaphore()
    ends = ((0, 0), (SEGMENTS - 1, nx - 1))
    before_last = 1.0 - relax_omega

    def field(f):
        return vol.at[0, pl.ds(SEGMENTS * f, SEGMENTS)]

    def before(step):
        return pots.at[step - 1] if step else out.at[1]

    def coefficients(k, _):
        for r in range(nx):
            gain = relax_omega / (6.0 + out[2, k, r])
            coef[k, r] = gain
            drive[k, r] = gain * drive[k, r]
        return 0

    def send_edges(phase):
        step = WIDE * phase
        for side, (k, r) in enumerate(ends):
            out_x[phase, side, 0] = pots[step, k, r]

        def pack(k, _):
            for r in range(nx):
                for side, y in enumerate((0, ny - 1)):
                    row = pots[step, k, r, y : y + 1, :]
                    out_y[phase, side, 0, pl.ds(k * nx + r, 1), :] = row
            return 0

        lax.fori_loop(0, SEGMENTS, pack, 0)
        parts = place_.edges(phase, out_x, out_y, in_x, in_y, 0, 1)
        copies = place_.exchange(phase, list(enumerate(parts)), send_sem, recv_sem)
        start(copies)
        return copies

    def send_rest(phase):
        step = WIDE * phase
        old = before(step)
        for side, (k, r) in enumerate(ends):
            out_x[phase, side, 1] = pots[step, k, r + 1 - 2 * side]
            out_x[phase, side, 2] = before_last * old[k, r] + drive[k, r]
            if phase == 0:
                out_x[phase, side, 3] = coef[k, r]
            for j, y in enumerate((0, ny - 1)):
                out_c[phase, 2 * side + j] = pots[step, k, r, y : y + 1, :]

        def pack(k, _):
            for r in range(nx):
                added = before_last * old[k, r] + drive[k, r]
                for side, y in enumerate((0, ny - 1)):
                    inward = y + 1 - 2 * side
                    rows = [pots[step, k, r, inward : inward + 1, :], added[y : y + 1]]
                    if phase == 0:
                        rows.append(coef[k, r, y : y + 1, :])
                    for f, row in enumerate(rows):
                        out_y[phase, side, 1 + f, pl.ds(k * nx + r, 1), :] = row
            return 0

        lax.fori_loop(0, SEGMENTS, pack, 0)
        parts = place_.edges(phase, out_x, out_y, in_x, in_y, 1, 3 if phase == 0 else 2)
        parts += place_.corners(phase, out_c, in_c)
        copies = place_.exchange(phase, list(enumerate(parts, 4)), send_sem, recv_sem)
        start(copies)
        return copies

    def sweep(step):
        old = before(step)

        def segment(k, _):
            planes = [pots[step, k, r] for r in range(nx)]
            below = jnp.where(k > 0, pots[step, jnp.maximum(k - 1, 0), nx - 1], 0.0)
            above = jnp.where(
                k < SEGMENTS - 1, pots[step, jnp.minimum(k + 1, SEGMENTS - 1), 0], 0.0
            )
            around = [below] + planes + [above]
            for r in range(nx):
                beside = around[r] + around[r + 2]
                beside += place_.beside_lines(planes[r], 0.0, 0.0)
                beside += place_.beside_z(planes[r], 0.0, 0.0)
                pots[step + 1, k, r] = drive[k, r] + before_last * old[k, r] + coef[k, r] * beside
            return 0

        lax.fori_loop(0, SEGMENTS, segment, 0)

    def correct(step, planes, rows):
        for side, (k, r) in enumerate(ends):
            beyond = jnp.where(place_.exists[0][side], planes[side][...], 0.0)
            pots[step + 1, k, r] += coef[k, r] * beyond

        def segment(k, _):
            low, high = (face[pl.ds(k * nx, nx), :] for face in rows)
            for r in range(nx):
                beyond = jnp.where(low_y, low[r : r + 1], 0.0)
                beyond += jnp.where(high_y, high[r : r + 1], 0.0)
                fresh = pots[step + 1, k, r] + coef[k, r] * beyond
                pots[step + 1, k, r] = fresh
                if step + 2 == STEPS:
                    out[1, k, r] = fresh
                if step + 1 == STEPS:
                    out[0, k, r] = fresh
            return 0

        lax.fori_loop(0, SEGMENTS, segment, 0)

    def step_ring(phase):
        step = WIDE * phase
        for side in range(2):
            cells = in_x[phase, side, 0]
            tips = [
                jnp.where(place_.exists[1][end], in_c[phase, 2 * side + end], 0.0)
                for end in range(2)
            ]
            beside = pots[step, *ends[side]] + in_x[phase, side, 1]
            beside += place_.beside_lines(cells, *tips) + place_.beside_z(cells, 0.0, 0.0)
            ring_x[phase, side] = in_x[phase, side, 2] + in_x[0, side, 3] * beside
        for side in range(2):
            tips = [
                jnp.where(place_.exists[0][end], in_c[phase, 2 * end + side], 0.0)
                for end in range(2)
            ]
            for k in range(SEGMENTS):
                rows = pl.ds(k * nx, nx)
                cells = in_y[phase, side, 0, rows, :]
                low = in_y[phase, side, 0, k * nx - 1 : k * nx, :] if k else tips[0]
                high = tips[1]
                if k + 1 < SEGMENTS:
                    high = in_y[phase, side, 0, (k + 1) * nx : (k + 1) * nx + 1, :]
                beside = out_y[phase, side, 0, rows, :] + in_y[phase, side, 1, rows, :]
                beside += place_.beside_lines(cells, low, high) + place_.beside_z(cells, 0.0, 0.0)
                ring_y[phase, side, rows, :] = (
                    in_y[phase, side, 2, rows, :] + in_y[0, side, 3, rows, :] * beside
                )

    def heart():
        pl.semaphore_wait(barrier, n_slab)
        n_ring = 4
        ring_size = n_slab // n_ring

        def send(i, _):
            there = ring_size * lax.rem(slab // ring_size + i, n_ring) + i // n_ring
            pltpu.make_async_remote_copy(
                src_ref=rows_out.at[there], dst_ref=rows_in.at[slab], send_sem=row_sem.at[0],
                recv_sem=row_sem.at[1], device_id=(1, there, col), device_id_type=MESH,
            ).start()
            return 0

        lax.fori_loop(0, n_slab, send, 0)
        wait_whole(rows_out, row_sem.at[0])

    def torso():
        loads = [
            load(field(0), pots.at[0], load_sem.at[0]),
            load(field(2), out.at[2], load_sem.at[1]),
            load(field(3), drive, load_sem.at[2]),
            load(field(1), out.at[1], load_sem.at[3]),
        ]
        place_.greet()

        def invite(i, _):
            there = (0, lax.rem(slab + i, n_slab), col)
            pl.semaphore_signal(barrier, inc=1, device_id=there, device_id_type=MESH)
            return 0

        lax.fori_loop(0, n_slab, invite, 0)
        loads[0].wait()
        place_.await_met()
        edges = send_edges(0)
        for copy in loads[1:]:
            copy.wait()
        lax.fori_loop(0, SEGMENTS, coefficients, 0)
        rest = send_rest(0)
        started = edges + rest
        for phase in range(PHASES):
            step = WIDE * phase
            sweep(step)
            wait_recv(edges)
            correct(
                step, [in_x.at[phase, side, 0] for side in range(2)],
                [in_y.at[phase, side, 0] for side in range(2)],
            )
            sweep(step + 1)
            wait_recv(rest)
            step_ring(phase)
            correct(
                step + 1, [ring_x.at[phase, side] for side in range(2)],
                [ring_y.at[phase, side] for side in range(2)],
            )
            if phase + 1 < PHASES:
                edges = send_edges(phase + 1)
                rest = send_rest(phase + 1)
                started += edges + rest

        wait_whole(rows_in, row_sem.at[1])
        wait_send(started)

    pl.when(place_.sec == 0)(heart)
    pl.when(place_.sec == 1)(torso)


def result_kernel(n_slab, state, fields, rows, out, inflow_ref, sems):
    nx, ny, nz = state.shape[1:]
    tx = SEGMENTS * nx
    sec = lax.axis_index("sec")

    def heart():
        load(state, out.at[0], sems.at[0]).wait()

    def torso():
        copies = [
            load(fields.at[f], out.at[0, pl.ds(SEGMENTS * f, SEGMENTS)], sems.at[f])
            for f in range(3)
        ]
        marks = jnp.where(
            iota((n_slab, LANES), 0) == iota((n_slab, LANES), 1) % n_slab, rows[:, 4, :], 0.0
        )
        marks = jnp.sum(marks, axis=0, keepdims=True)[:, : CAP * n_slab]
        goals = iota((tx * ny, CAP * n_slab), 0).astype(jnp.float32)
        hits = (goals == marks).astype(jnp.float32).astype(jnp.bfloat16)
        got = jnp.concatenate(
            [
                jnp.concatenate([rows[:, 2 * r + h, :] for r in range(CAP)], axis=0)
                for h in range(2)
            ],
            axis=1,
        )
        inflow = matmul(jnp.concatenate([hits, hits], axis=1), split_halves(got), ((1,), (0,)))
        inflow_ref[...] = inflow.reshape(SEGMENTS, nx, ny, nz)
        copies.append(load(inflow_ref, out.at[0, pl.ds(3 * SEGMENTS, SEGMENTS)], sems.at[3]))
        for copy in copies:
            copy.wait()

    pl.when(sec == 0)(heart)
    pl.when(sec == 1)(torso)


def solution(mesh):
    n_slab, n_col = mesh.shape["slab"], mesh.shape["col"]

    def on_device(volume, epi_line, epi_dest, epi_target):
        _, fields, nx, ny, nz = volume.shape
        epi = epi_line.shape[-1]
        tx = SEGMENTS * nx
        f32, dma = jnp.float32, pltpu.SemaphoreType.DMA
        fields_type = jax.ShapeDtypeStruct((fields, nx, ny, nz), f32)
        volume, epi_line, epi_dest, epi_target = (
            pltpu.with_memory_space_constraint(x, pltpu.HBM)
            for x in (volume, epi_line, epi_dest.reshape(epi_line.shape), epi_target)
        )
        hbm = pl.BlockSpec(memory_space=pltpu.HBM)
        vmem = pl.BlockSpec(memory_space=pltpu.VMEM)
        state, rows = pl.pallas_call(
            functools.partial(heart_kernel, n_slab, n_col),
            out_shape=(fields_type, jax.ShapeDtypeStruct((n_slab, 5, LANES), f32)),
            in_specs=[hbm] * 4,
            out_specs=(vmem, vmem),
            scratch_shapes=[
                pltpu.VMEM((STEPS + 1, nx, ny, nz), f32),
                pltpu.VMEM((2, nx, ny, nz), f32),
                pltpu.VMEM((PHASES, 2, 5, ny, nz), f32),
                pltpu.VMEM((PHASES, 2, 5, nx, nz), f32),
                pltpu.VMEM((PHASES, 4, 1, nz), f32),
                pltpu.VMEM((PHASES, 2, 5, ny, nz), f32),
                pltpu.VMEM((PHASES, 2, 5, nx, nz), f32),
                pltpu.VMEM((PHASES, 4, 1, nz), f32),
                pltpu.VMEM((PHASES, 4, ny, nz), f32),
                pltpu.VMEM((4 * n_slab, 4 * nx * ny), jnp.bfloat16),
                pltpu.VMEM((3, 1, epi), jnp.int32),
                dma((2,)), dma((3,)), dma((PHASES, 12)), dma((PHASES, 12)),
            ],
            compiler_params=pltpu.CompilerParams(
                collective_id=0, has_side_effects=True, vmem_limit_bytes=VMEM_LIMIT
            ),
        )(volume, epi_line, epi_dest, epi_target)
        fields, got = pl.pallas_call(
            functools.partial(torso_kernel, n_slab, n_col),
            out_shape=(
                jax.ShapeDtypeStruct((3, SEGMENTS, nx, ny, nz), f32),
                jax.ShapeDtypeStruct((n_slab, 5, LANES), f32),
            ),
            in_specs=[hbm, vmem],
            out_specs=(vmem, vmem),
            scratch_shapes=[
                pltpu.VMEM((STEPS + 1, SEGMENTS, nx, ny, nz), f32),
                pltpu.VMEM((SEGMENTS, nx, ny, nz), f32),
                pltpu.VMEM((SEGMENTS, nx, ny, nz), f32),
                pltpu.VMEM((PHASES, 2, 4, ny, nz), f32),
                pltpu.VMEM((PHASES, 2, 4, tx, nz), f32),
                pltpu.VMEM((PHASES, 4, 1, nz), f32),
                pltpu.VMEM((PHASES, 2, 4, ny, nz), f32),
                pltpu.VMEM((PHASES, 2, 4, tx, nz), f32),
                pltpu.VMEM((PHASES, 4, 1, nz), f32),
                pltpu.VMEM((PHASES, 2, ny, nz), f32),
                pltpu.VMEM((PHASES, 2, tx, nz), f32),
                dma((4,)), dma((PHASES, 12)), dma((PHASES, 12)), dma((2,)),
            ],
            compiler_params=pltpu.CompilerParams(
                collective_id=1, has_side_effects=True, vmem_limit_bytes=VMEM_LIMIT
            ),
        )(volume, rows)
        return pl.pallas_call(
            functools.partial(result_kernel, n_slab),
            out_shape=jax.ShapeDtypeStruct(volume.shape, f32),
            in_specs=[vmem, vmem, vmem],
            out_specs=hbm,
            scratch_shapes=[pltpu.VMEM((SEGMENTS, nx, ny, nz), f32), dma((4,))],
            compiler_params=pltpu.CompilerParams(vmem_limit_bytes=VMEM_LIMIT),
        )(state, fields, got)

    return jax.shard_map(
        on_device,
        mesh=mesh,
        in_specs=(
            P("sec", None, "slab", "col", None),
            P("slab", "col", None),
            P("slab", "col", None, None),
            P("slab", "col", None),
        ),
        out_specs=P("sec", None, "slab", "col", None),
        check_vma=False,
    )
```

time: 39.1 us -> 33.1 us (0.85)
  Pallas kernels: 37.8 us -> 32.7 us
  local copies, waits for them, and re-layouts: 1.06 us -> 0 us
    pallas_call x1, Pallas kernels: 36.8 us -> 30.4 us  [on_device(): pl.pallas_call(functools.partial(torso_kernel, n_slab, n_col), out_shape=...]
    pallas_call x0 -> x1, Pallas kernels: none -> 1.16 us  [on_device(): pl.pallas_call(functools.partial(result_kernel, n_slab), out_shape=jax.Sh...]
    unnamed x1 -> x0, local copies, waits for them, and re-layouts: 1.06 us -> none
where the time goes in v3:
time: 33.1 us; the launch traced here: 32.7 us
  Pallas kernels  32.7 us (99%)
    pallas_call x1, Pallas kernels, on_device(): pl.pallas_call(functools.partial(torso_kernel, n_slab, n_col), out_shape=...  30.4 us
    pallas_call x1, Pallas kernels, on_device(): pl.pallas_call(functools.partial(heart_kernel, n_slab, n_col), out_shape=...  1.18 us
    pallas_call x1, Pallas kernels, on_device(): pl.pallas_call(functools.partial(result_kernel, n_slab), out_shape=jax.Sh...  1.16 us

profile of v3, /device:TPU:24, one launch (start us, length us, event | category | flops | bytes accessed | tf_op | source)
XLA Modules:
  0.0 32.7 jit_solution(3022218021464617713)
XLA Ops:
  0.0 1.2 %shard_map.46 = (f32[20,8,8,256]{3,2,1,0:T(8,128)S(1)}, f32[64,5,128]{2,1,0:T(8,128)S(1)}) custom-call(f32[1,20,8,8,256]{4,3,2,1,0:T(8,128)} %vol.3, s32[1,1,64]{2,1,0:T(1,128)} %line_hbm.1, s32[1,1,64]{2,1,0:T(1,128)} %bitcast.1, s32[1,1,64]{2,1,0:T(1,128)} %target_hbm.1), custom_call_target="tpu_custom_call" | custom-call | tf_op jit(solution)/shard_map/pallas_call | solution.py:622
  1.2 30.4 %shard_map.47 = (f32[3,5,8,8,256]{4,3,2,1,0:T(8,128)S(1)}, f32[64,5,128]{2,1,0:T(8,128)S(1)}) custom-call(f32[1,20,8,8,256]{4,3,2,1,0:T(8,128)} %vol.3, f32[64,5,128]{2,1,0:T(8,128)S(1)} %get-tuple-element.10.rows_out), custom_call_target="tpu_custom_call" | custom-call | tf_op jit(solution)/shard_map/pallas_call | solution.py:645
  31.5 1.2 %shard_map.48 = f32[1,20,8,8,256]{4,3,2,1,0:T(8,128)} custom-call(f32[20,8,8,256]{3,2,1,0:T(8,128)S(1)} %get-tuple-element.9.state, f32[3,5,8,8,256]{4,3,2,1,0:T(8,128)S(1)} %get-tuple-element.11.fields, f32[64,5,128]{2,1,0:T(8,128)S(1)} %get-tuple-element.12.rows), custom_call_target="tpu_custom_call" | custom-call | tf_op jit(solution)/shard_map/pallas_call | solution.py:671

commit v4 on v3

--- a/solution.py
+++ b/solution.py
@@ -12,7 +12,9 @@
 CAP = 2
 GATES = 18
 LANES = 128
+NARROW = 8
 SEGMENTS = 5
+N_RING = 4
 WIDE = 2
 PHASES = STEPS // WIDE
 VMEM_LIMIT = 24 * 1024 * 1024
@@ -45,6 +47,7 @@
 class Place:
     def __init__(self, n_slab, n_col, sizes):
         self.n_slab, self.n_col = n_slab, n_col
+        self.ring_size = n_slab // N_RING
         self.sec = sec = lax.axis_index("sec")
         self.slab = slab = lax.axis_index("slab")
         self.col = col = lax.axis_index("col")
@@ -62,8 +65,14 @@
         self.met += [(exists[0][i], (sec, slab + 2 * i - 1, col)) for i in range(2)]
         self.met += [(exists[1][j], (sec, slab, col + 2 * j - 1)) for j in range(2)]
 
-    def greet(self):
-        for here, there in self.met:
+    def across(self, sec):
+        return [
+            (self.slab >= 0, (sec, lax.rem(self.slab + i * self.ring_size, self.n_slab), self.col))
+            for i in range(N_RING)
+        ]
+
+    def greet(self, others):
+        for here, there in self.met[4:] + others + self.met[:4]:
 
             @pl.when(here)
             def _(there=there):
@@ -71,8 +80,8 @@
                     pltpu.get_barrier_semaphore(), inc=1, device_id=there, device_id_type=MESH
                 )
 
-    def await_met(self):
-        count = sum(here.astype(jnp.int32) for here, _ in self.met)
+    def await_met(self, others=()):
+        count = sum(here.astype(jnp.int32) for here, _ in [*self.met, *others])
         pl.semaphore_wait(pltpu.get_barrier_semaphore(), count)
 
     def exchange(self, phase, parts, send_sem, recv_sem):
@@ -80,7 +89,7 @@
         for way, (direction, src, dst) in parts:
             here, there = self.met[direction]
             copy = pltpu.make_async_remote_copy(
-                src_ref=src, dst_ref=dst, send_sem=send_sem.at[phase, way],
+                src_ref=src, dst_ref=dst, send_sem=send_sem.at[way],
                 recv_sem=recv_sem.at[phase, way], device_id=there, device_id_type=MESH,
             )
             copies.append((here, copy, self.met[(3, 2, 1, 0, 5, 4, 7, 6)[direction]][0]))
@@ -133,13 +142,12 @@
     pltpu.make_async_copy(ref, ref, sem).wait()
 
 
-def heart_kernel(
-    n_slab, n_col,
-    vol, line_hbm, dest_hbm, target_hbm, state, rows_out,
-    pots, moments, out_x, out_y, out_c, in_x, in_y, in_c, ring, picks, meta,
-    load_sem, meta_sem, send_sem, recv_sem,
+def heart_part(
+    place_, vol, line_hbm, dest_hbm, target_hbm, state, rows_in, lines_in,
+    pots, moments, out_x, out_y, out_c, in_x, in_y, in_c, ring, picks, meta, rows_out, lines_out,
+    meta_sem, send_sem, recv_sem, row_sem, ready_sem,
 ):
-    place_ = Place(n_slab, n_col, vol.shape)
+    n_slab, slab, col = place_.n_slab, place_.slab, place_.col
     low_y, high_y = place_.low_y, place_.high_y
     nx, ny, nz = vol.shape[2:]
     ends_x, ends_y = (0, nx - 1), (0, ny - 1)
@@ -268,21 +276,20 @@
 
     def heart():
         loads = [
-            load(vol.at[0, 0], pots.at[0], load_sem.at[0]),
-            load(vol.at[0, pl.ds(1, GATES + 1)], state.at[pl.ds(1, GATES + 1)], load_sem.at[1]),
+            load(vol.at[0, 0], pots.at[0], send_sem.at[4]),
+            load(vol.at[0, pl.ds(1, GATES + 1)], state.at[pl.ds(1, GATES + 1)], send_sem.at[5]),
         ]
         metas = [
             load(src.at[0], meta.at[i], meta_sem.at[i])
             for i, src in enumerate((line_hbm, dest_hbm, target_hbm))
         ]
-        place_.greet()
+        place_.greet(place_.across(1))
         loads[0].wait()
         place_.await_met()
         edges = send_edges(0)
         loads[1].wait()
         lax.fori_loop(0, nx, first_moments, 0, unroll=2)
         rest = send_rest(0)
-        started = edges + rest
 
         for copy in metas:
             copy.wait()
@@ -313,16 +320,30 @@
                 [ring.at[phase, 2 + side] for side in range(2)],
             )
             if phase + 1 < PHASES:
+                wait_send(edges + rest)
                 edges = send_edges(phase + 1)
                 rest = send_rest(phase + 1)
-                started += edges + rest
 
         state[0] = pots[STEPS]
         final = pots[STEPS].reshape(lines, nz)
         source = jnp.concatenate([final[:, :LANES], final[:, LANES:]], axis=0)
         rows = matmul(picks[...], split_halves(source), ((1,), (0,)))
-        rows_out[:, :4, :] = rows.reshape(n_slab, 4, LANES)
-        wait_send(started)
+        rows_out[...] = rows.reshape(n_slab, 4, LANES)
+        pl.semaphore_wait(ready_sem, N_RING)
+
+        def send(i, _):
+            there = place_.ring_size * lax.rem(i, N_RING) + i // N_RING
+            for f, (src, dst) in enumerate(((rows_out, rows_in), (lines_out, lines_in))):
+                pltpu.make_async_remote_copy(
+                    src_ref=src.at[there], dst_ref=dst.at[slab], send_sem=row_sem.at[f, 0],
+                    recv_sem=row_sem.at[f, 1], device_id=(1, there, col), device_id_type=MESH,
+                ).start()
+            return 0
+
+        lax.fori_loop(0, n_slab, send, 0)
+        wait_whole(rows_out, row_sem.at[0, 0])
+        wait_whole(lines_out, row_sem.at[1, 0])
+        wait_send(edges + rest)
 
     def fill_picks(lines):
         epi = meta.shape[2]
@@ -352,24 +373,20 @@
             chosen = jnp.logical_and(marks_d, rank_d == float(r))
             goal = jnp.where(chosen, (target + 1).astype(jnp.float32), 0.0)
             goals.append(jnp.sum(goal, axis=1, keepdims=True) - 1.0)
-        lane_s = iota((n_slab, LANES), 1)
-        rows_out[:, 4, :] = jnp.where(lane_s < n_slab, goals[0], goals[1])
-
-    pl.when(place_.sec == 0)(heart)
-
-
-def torso_kernel(
-    n_slab, n_col,
-    vol, rows_out, out, rows_in,
+        lines_out[:, 0, :] = jnp.where(iota((n_slab, NARROW), 1) == 0, goals[0], goals[1])
+
+    heart()
+
+
+def torso_part(
+    place_, vol, out, rows_in, lines_in,
     pots, coef, drive, out_x, out_y, out_c, in_x, in_y, in_c, ring_x, ring_y,
-    load_sem, send_sem, recv_sem, row_sem,
+    send_sem, recv_sem, row_sem, ready_sem, round_sem,
 ):
-    place_ = Place(n_slab, n_col, vol.shape)
-    slab, col = place_.slab, place_.col
+    n_slab, slab, col = place_.n_slab, place_.slab, place_.col
     low_y, high_y = place_.low_y, place_.high_y
     nx, ny, nz = vol.shape[2:]
     tx = SEGMENTS * nx
-    barrier = pltpu.get_barrier_semaphore()
     ends = ((0, 0), (SEGMENTS - 1, nx - 1))
     before_last = 1.0 - relax_omega
 
@@ -502,45 +519,42 @@
                     in_y[phase, side, 2, rows, :] + in_y[0, side, 3, rows, :] * beside
                 )
 
-    def heart():
-        pl.semaphore_wait(barrier, n_slab)
-        n_ring = 4
-        ring_size = n_slab // n_ring
-
-        def send(i, _):
-            there = ring_size * lax.rem(slab // ring_size + i, n_ring) + i // n_ring
-            pltpu.make_async_remote_copy(
-                src_ref=rows_out.at[there], dst_ref=rows_in.at[slab], send_sem=row_sem.at[0],
-                recv_sem=row_sem.at[1], device_id=(1, there, col), device_id_type=MESH,
-            ).start()
-            return 0
-
-        lax.fori_loop(0, n_slab, send, 0)
-        wait_whole(rows_out, row_sem.at[0])
-
     def torso():
         loads = [
-            load(field(0), pots.at[0], load_sem.at[0]),
-            load(field(2), out.at[2], load_sem.at[1]),
-            load(field(3), drive, load_sem.at[2]),
-            load(field(1), out.at[1], load_sem.at[3]),
-        ]
-        place_.greet()
-
-        def invite(i, _):
-            there = (0, lax.rem(slab + i, n_slab), col)
-            pl.semaphore_signal(barrier, inc=1, device_id=there, device_id_type=MESH)
-            return 0
-
-        lax.fori_loop(0, n_slab, invite, 0)
+            load(field(0), pots.at[0], send_sem.at[4]),
+            load(field(2), out.at[2], send_sem.at[5]),
+            load(field(3), drive, send_sem.at[6]),
+            load(field(1), out.at[1], send_sem.at[7]),
+        ]
+        ring_size = place_.ring_size
+        at = lax.rem(slab, ring_size)
+
+        def along(k):
+            return (1, slab - at + lax.rem(at + k + ring_size, ring_size), col)
+
+        others = []
+        reach = ring_size // 4
+        if reach:
+            others += [(at == 0, along(-1)), (at == ring_size - 1, along(1))]
+        for k in range(2, reach + 1):
+            others += [(slab >= 0, along(k)), (slab >= 0, along(-k))]
+        place_.greet(others)
+
+        hearts = place_.across(0)
+        place_.await_met(others + hearts)
+        if reach:
+            for k in (reach, -reach):
+                pl.semaphore_signal(round_sem, inc=1, device_id=along(k), device_id_type=MESH)
         loads[0].wait()
-        place_.await_met()
         edges = send_edges(0)
         for copy in loads[1:]:
             copy.wait()
         lax.fori_loop(0, SEGMENTS, coefficients, 0)
         rest = send_rest(0)
-        started = edges + rest
+        if reach:
+            pl.semaphore_wait(round_sem, 2)
+        for _, there in hearts:
+            pl.semaphore_signal(ready_sem, inc=1, device_id=there, device_id_type=MESH)
         for phase in range(PHASES):
             step = WIDE * phase
             sweep(step)
@@ -557,18 +571,39 @@
                 [ring_y.at[phase, side] for side in range(2)],
             )
             if phase + 1 < PHASES:
+                wait_send(edges + rest)
                 edges = send_edges(phase + 1)
                 rest = send_rest(phase + 1)
-                started += edges + rest
-
-        wait_whole(rows_in, row_sem.at[1])
-        wait_send(started)
-
-    pl.when(place_.sec == 0)(heart)
-    pl.when(place_.sec == 1)(torso)
-
-
-def result_kernel(n_slab, state, fields, rows, out, inflow_ref, sems):
+
+        wait_whole(rows_in, row_sem.at[0, 1])
+        wait_whole(lines_in, row_sem.at[1, 1])
+        wait_send(edges + rest)
+
+    torso()
+
+
+def main_kernel(n_slab, n_col, heart_refs, torso_refs, *refs):
+    vol, line, dest, target, state, fields, rows_in, lines_in, *scratch = refs
+    own_heart, own_torso = scratch[:heart_refs], scratch[heart_refs : heart_refs + torso_refs]
+    meta_sem, send_sem, recv_sem, row_sem, ready_sem, round_sem = scratch[heart_refs + torso_refs :]
+    place_ = Place(n_slab, n_col, vol.shape)
+
+    @pl.when(place_.sec == 0)
+    def _():
+        heart_part(
+            place_, vol, line, dest, target, state, rows_in, lines_in, *own_heart,
+            meta_sem, send_sem, recv_sem, row_sem, ready_sem,
+        )
+
+    @pl.when(place_.sec == 1)
+    def _():
+        torso_part(
+            place_, vol, fields, rows_in, lines_in, *own_torso,
+            send_sem, recv_sem, row_sem, ready_sem, round_sem,
+        )
+
+
+def result_kernel(n_slab, state, fields, rows, lines, out, inflow_ref, sems):
     nx, ny, nz = state.shape[1:]
     tx = SEGMENTS * nx
     sec = lax.axis_index("sec")
@@ -581,10 +616,10 @@
             load(fields.at[f], out.at[0, pl.ds(SEGMENTS * f, SEGMENTS)], sems.at[f])
             for f in range(3)
         ]
-        marks = jnp.where(
-            iota((n_slab, LANES), 0) == iota((n_slab, LANES), 1) % n_slab, rows[:, 4, :], 0.0
-        )
-        marks = jnp.sum(marks, axis=0, keepdims=True)[:, : CAP * n_slab]
+        slots = (n_slab, CAP * n_slab)
+        goal = jnp.where(iota(slots, 1) < n_slab, lines[:, 0, 0:1], lines[:, 0, 1:2])
+        marks = jnp.where(iota(slots, 0) == iota(slots, 1) % n_slab, goal, 0.0)
+        marks = jnp.sum(marks, axis=0, keepdims=True)
         goals = iota((tx * ny, CAP * n_slab), 0).astype(jnp.float32)
         hits = (goals == marks).astype(jnp.float32).astype(jnp.bfloat16)
         got = jnp.concatenate(
@@ -612,19 +647,13 @@
         epi = epi_line.shape[-1]
         tx = SEGMENTS * nx
         f32, dma = jnp.float32, pltpu.SemaphoreType.DMA
-        fields_type = jax.ShapeDtypeStruct((fields, nx, ny, nz), f32)
         volume, epi_line, epi_dest, epi_target = (
             pltpu.with_memory_space_constraint(x, pltpu.HBM)
             for x in (volume, epi_line, epi_dest.reshape(epi_line.shape), epi_target)
         )
         hbm = pl.BlockSpec(memory_space=pltpu.HBM)
         vmem = pl.BlockSpec(memory_space=pltpu.VMEM)
-        state, rows = pl.pallas_call(
-            functools.partial(heart_kernel, n_slab, n_col),
-            out_shape=(fields_type, jax.ShapeDtypeStruct((n_slab, 5, LANES), f32)),
-            in_specs=[hbm] * 4,
-            out_specs=(vmem, vmem),
-            scratch_shapes=[
+        heart_scratch = [
                 pltpu.VMEM((STEPS + 1, nx, ny, nz), f32),
                 pltpu.VMEM((2, nx, ny, nz), f32),
                 pltpu.VMEM((PHASES, 2, 5, ny, nz), f32),
@@ -636,21 +665,10 @@
                 pltpu.VMEM((PHASES, 4, ny, nz), f32),
                 pltpu.VMEM((4 * n_slab, 4 * nx * ny), jnp.bfloat16),
                 pltpu.VMEM((3, 1, epi), jnp.int32),
-                dma((2,)), dma((3,)), dma((PHASES, 12)), dma((PHASES, 12)),
-            ],
-            compiler_params=pltpu.CompilerParams(
-                collective_id=0, has_side_effects=True, vmem_limit_bytes=VMEM_LIMIT
-            ),
-        )(volume, epi_line, epi_dest, epi_target)
-        fields, got = pl.pallas_call(
-            functools.partial(torso_kernel, n_slab, n_col),
-            out_shape=(
-                jax.ShapeDtypeStruct((3, SEGMENTS, nx, ny, nz), f32),
-                jax.ShapeDtypeStruct((n_slab, 5, LANES), f32),
-            ),
-            in_specs=[hbm, vmem],
-            out_specs=(vmem, vmem),
-            scratch_shapes=[
+                pltpu.VMEM((n_slab, 4, LANES), f32),
+                pltpu.VMEM((n_slab, 1, NARROW), f32),
+        ]
+        torso_scratch = [
                 pltpu.VMEM((STEPS + 1, SEGMENTS, nx, ny, nz), f32),
                 pltpu.VMEM((SEGMENTS, nx, ny, nz), f32),
                 pltpu.VMEM((SEGMENTS, nx, ny, nz), f32),
@@ -662,20 +680,36 @@
                 pltpu.VMEM((PHASES, 4, 1, nz), f32),
                 pltpu.VMEM((PHASES, 2, ny, nz), f32),
                 pltpu.VMEM((PHASES, 2, tx, nz), f32),
-                dma((4,)), dma((PHASES, 12)), dma((PHASES, 12)), dma((2,)),
+        ]
+        regular = pltpu.SemaphoreType.REGULAR
+        state, fields, rows, lines = pl.pallas_call(
+            functools.partial(
+                main_kernel, n_slab, n_col, len(heart_scratch), len(torso_scratch)
+            ),
+            out_shape=(
+                jax.ShapeDtypeStruct((fields, nx, ny, nz), f32),
+                jax.ShapeDtypeStruct((3, SEGMENTS, nx, ny, nz), f32),
+                jax.ShapeDtypeStruct((n_slab, 4, LANES), f32),
+                jax.ShapeDtypeStruct((n_slab, 1, NARROW), f32),
+            ),
+            in_specs=[hbm] * 4,
+            out_specs=(vmem,) * 4,
+            scratch_shapes=[
+                *heart_scratch, *torso_scratch,
+                dma((3,)), dma((12,)), dma((PHASES, 12)), dma((2, 2)), regular, regular,
             ],
             compiler_params=pltpu.CompilerParams(
-                collective_id=1, has_side_effects=True, vmem_limit_bytes=VMEM_LIMIT
+                collective_id=0, has_side_effects=True, vmem_limit_bytes=VMEM_LIMIT
             ),
-        )(volume, rows)
+        )(volume, epi_line, epi_dest, epi_target)
         return pl.pallas_call(
             functools.partial(result_kernel, n_slab),
             out_shape=jax.ShapeDtypeStruct(volume.shape, f32),
-            in_specs=[vmem, vmem, vmem],
+            in_specs=[vmem, vmem, vmem, vmem],
             out_specs=hbm,
             scratch_shapes=[pltpu.VMEM((SEGMENTS, nx, ny, nz), f32), dma((4,))],
             compiler_params=pltpu.CompilerParams(vmem_limit_bytes=VMEM_LIMIT),
-        )(state, fields, got)
+        )(state, fields, rows, lines)
 
     return jax.shard_map(
         on_device,

time: 33.1 us -> 31.4 us (0.949)
  the two profiles are of different devices: /device:TPU:24 before, /device:TPU:80 now
where the time goes in v4:
time: 31.4 us; the launch traced here: 31.3 us
  Pallas kernels  31.3 us (100%)
    pallas_call x1, Pallas kernels, on_device(): pl.pallas_call(functools.partial(main_kernel, n_slab, n_col, len(heart_sc...  30.1 us
    pallas_call x1, Pallas kernels, on_device(): pl.pallas_call(functools.partial(result_kernel, n_slab), out_shape=jax.Sh...  1.2 us

profile of v4, /device:TPU:80, one launch (start us, length us, event | category | flops | bytes accessed | tf_op | source)
XLA Modules:
  0.0 31.3 jit_solution(2344362100595026847)
XLA Ops:
  0.0 30.1 %shard_map.46 = (f32[20,8,8,256]{3,2,1,0:T(8,128)S(1)}, f32[3,5,8,8,256]{4,3,2,1,0:T(8,128)S(1)}, f32[64,4,128]{2,1,0:T(4,128)S(1)}, f32[64,1,8]{2,1,0:T(1,128)S(1)}) custom-call(f32[1,20,8,8,256]{4,3,2,1,0:T(8,128)} %refs_0_.1, s32[1,1,64]{2,1,0:T(1,128)} %refs_1_.1, s32[1,1,64]{2,1,0:T(1,128)} %bitcast.1, s32[1,1,64]{2,1,0:T(1,128)} %refs_3_.1), custom_call_target="tpu_custom_call" | custom-call | tf_op jit(solution)/shard_map/pallas_call | solution.py:685
  30.1 1.2 %shard_map.47 = f32[1,20,8,8,256]{4,3,2,1,0:T(8,128)} custom-call(f32[20,8,8,256]{3,2,1,0:T(8,128)S(1)} %get-tuple-element.9.state, f32[3,5,8,8,256]{4,3,2,1,0:T(8,128)S(1)} %get-tuple-element.10.fields, f32[64,4,128]{2,1,0:T(4,128)S(1)} %get-tuple-element.11.rows, f32[64,1,8]{2,1,0:T(1,128)S(1)} %get-tuple-element.12.lines), custom_call_target="tpu_custom_call" | custom-call | tf_op jit(solution)/shard_map/pallas_call | solution.py:705

commit v5 on v4

--- a/solution.py
+++ b/solution.py
@@ -274,6 +274,17 @@
     def in_sigma(axis, side):
         return (in_x, in_y)[axis][0, side, 4]
 
+    def to_all(src, dst, which):
+        def send(i, _):
+            there = place_.ring_size * lax.rem(i, N_RING) + i // N_RING
+            pltpu.make_async_remote_copy(
+                src_ref=src.at[there], dst_ref=dst.at[slab], send_sem=row_sem.at[which, 0],
+                recv_sem=row_sem.at[which, 1], device_id=(1, there, col), device_id_type=MESH,
+            ).start()
+            return 0
+
+        lax.fori_loop(0, n_slab, send, 0)
+
     def heart():
         loads = [
             load(vol.at[0, 0], pots.at[0], send_sem.at[4]),
@@ -307,6 +318,9 @@
                 return 0
 
             lax.fori_loop(0, nx, first, 0, unroll=2)
+            if phase + 1 == PHASES:
+                pl.semaphore_wait(ready_sem, N_RING)
+                to_all(lines_out, lines_in, 1)
             wait_recv(edges)
             correct(
                 step, [in_x.at[phase, side, 0] for side in range(2)],
@@ -329,18 +343,7 @@
         source = jnp.concatenate([final[:, :LANES], final[:, LANES:]], axis=0)
         rows = matmul(picks[...], split_halves(source), ((1,), (0,)))
         rows_out[...] = rows.reshape(n_slab, 4, LANES)
-        pl.semaphore_wait(ready_sem, N_RING)
-
-        def send(i, _):
-            there = place_.ring_size * lax.rem(i, N_RING) + i // N_RING
-            for f, (src, dst) in enumerate(((rows_out, rows_in), (lines_out, lines_in))):
-                pltpu.make_async_remote_copy(
-                    src_ref=src.at[there], dst_ref=dst.at[slab], send_sem=row_sem.at[f, 0],
-                    recv_sem=row_sem.at[f, 1], device_id=(1, there, col), device_id_type=MESH,
-                ).start()
-            return 0
-
-        lax.fori_loop(0, n_slab, send, 0)
+        to_all(rows_out, rows_in, 0)
         wait_whole(rows_out, row_sem.at[0, 0])
         wait_whole(lines_out, row_sem.at[1, 0])
         wait_send(edges + rest)
@@ -379,9 +382,9 @@
 
 
 def torso_part(
-    place_, vol, out, rows_in, lines_in,
+    place_, vol, out, rows_in, hits_ref, lines_in,
     pots, coef, drive, out_x, out_y, out_c, in_x, in_y, in_c, ring_x, ring_y,
-    send_sem, recv_sem, row_sem, ready_sem, round_sem,
+    send_sem, recv_sem, row_sem, ready_sem,
 ):
     n_slab, slab, col = place_.n_slab, place_.slab, place_.col
     low_y, high_y = place_.low_y, place_.high_y
@@ -533,28 +536,22 @@
             return (1, slab - at + lax.rem(at + k + ring_size, ring_size), col)
 
         others = []
-        reach = ring_size // 4
-        if reach:
+        if ring_size > 2:
             others += [(at == 0, along(-1)), (at == ring_size - 1, along(1))]
-        for k in range(2, reach + 1):
-            others += [(slab >= 0, along(k)), (slab >= 0, along(-k))]
+        for k in sorted(range(2, ring_size - 1), key=lambda k: -min(k, ring_size - k)):
+            others.append((slab >= 0, along(k)))
         place_.greet(others)
 
         hearts = place_.across(0)
         place_.await_met(others + hearts)
-        if reach:
-            for k in (reach, -reach):
-                pl.semaphore_signal(round_sem, inc=1, device_id=along(k), device_id_type=MESH)
+        for _, there in hearts:
+            pl.semaphore_signal(ready_sem, inc=1, device_id=there, device_id_type=MESH)
         loads[0].wait()
         edges = send_edges(0)
         for copy in loads[1:]:
             copy.wait()
         lax.fori_loop(0, SEGMENTS, coefficients, 0)
         rest = send_rest(0)
-        if reach:
-            pl.semaphore_wait(round_sem, 2)
-        for _, there in hearts:
-            pl.semaphore_signal(ready_sem, inc=1, device_id=there, device_id_type=MESH)
         for phase in range(PHASES):
             step = WIDE * phase
             sweep(step)
@@ -575,17 +572,25 @@
                 edges = send_edges(phase + 1)
                 rest = send_rest(phase + 1)
 
+        wait_whole(lines_in, row_sem.at[1, 1])
+        slots = (n_slab, CAP * n_slab)
+        goal = jnp.where(iota(slots, 1) < n_slab, lines_in[:, 0, 0:1], lines_in[:, 0, 1:2])
+        marks = jnp.where(iota(slots, 0) == iota(slots, 1) % n_slab, goal, 0.0)
+        marks = jnp.sum(marks, axis=0, keepdims=True)
+        goals = iota((tx * ny, CAP * n_slab), 0).astype(jnp.float32)
+        hits = (goals == marks).astype(jnp.float32).astype(jnp.bfloat16)
+        hits_ref[:, : CAP * n_slab] = hits
+        hits_ref[:, CAP * n_slab :] = hits
         wait_whole(rows_in, row_sem.at[0, 1])
-        wait_whole(lines_in, row_sem.at[1, 1])
         wait_send(edges + rest)
 
     torso()
 
 
 def main_kernel(n_slab, n_col, heart_refs, torso_refs, *refs):
-    vol, line, dest, target, state, fields, rows_in, lines_in, *scratch = refs
+    vol, line, dest, target, state, fields, rows_in, hits, lines_in, *scratch = refs
     own_heart, own_torso = scratch[:heart_refs], scratch[heart_refs : heart_refs + torso_refs]
-    meta_sem, send_sem, recv_sem, row_sem, ready_sem, round_sem = scratch[heart_refs + torso_refs :]
+    meta_sem, send_sem, recv_sem, row_sem, ready_sem = scratch[heart_refs + torso_refs :]
     place_ = Place(n_slab, n_col, vol.shape)
 
     @pl.when(place_.sec == 0)
@@ -598,12 +603,12 @@
     @pl.when(place_.sec == 1)
     def _():
         torso_part(
-            place_, vol, fields, rows_in, lines_in, *own_torso,
-            send_sem, recv_sem, row_sem, ready_sem, round_sem,
+            place_, vol, fields, rows_in, hits, lines_in, *own_torso,
+            send_sem, recv_sem, row_sem, ready_sem,
         )
 
 
-def result_kernel(n_slab, state, fields, rows, lines, out, inflow_ref, sems):
+def result_kernel(state, fields, rows, hits, out, inflow_ref, sems):
     nx, ny, nz = state.shape[1:]
     tx = SEGMENTS * nx
     sec = lax.axis_index("sec")
@@ -616,12 +621,6 @@
             load(fields.at[f], out.at[0, pl.ds(SEGMENTS * f, SEGMENTS)], sems.at[f])
             for f in range(3)
         ]
-        slots = (n_slab, CAP * n_slab)
-        goal = jnp.where(iota(slots, 1) < n_slab, lines[:, 0, 0:1], lines[:, 0, 1:2])
-        marks = jnp.where(iota(slots, 0) == iota(slots, 1) % n_slab, goal, 0.0)
-        marks = jnp.sum(marks, axis=0, keepdims=True)
-        goals = iota((tx * ny, CAP * n_slab), 0).astype(jnp.float32)
-        hits = (goals == marks).astype(jnp.float32).astype(jnp.bfloat16)
         got = jnp.concatenate(
             [
                 jnp.concatenate([rows[:, 2 * r + h, :] for r in range(CAP)], axis=0)
@@ -629,7 +628,7 @@
             ],
             axis=1,
         )
-        inflow = matmul(jnp.concatenate([hits, hits], axis=1), split_halves(got), ((1,), (0,)))
+        inflow = matmul(hits[...], split_halves(got), ((1,), (0,)))
         inflow_ref[...] = inflow.reshape(SEGMENTS, nx, ny, nz)
         copies.append(load(inflow_ref, out.at[0, pl.ds(3 * SEGMENTS, SEGMENTS)], sems.at[3]))
         for copy in copies:
@@ -682,7 +681,7 @@
                 pltpu.VMEM((PHASES, 2, tx, nz), f32),
         ]
         regular = pltpu.SemaphoreType.REGULAR
-        state, fields, rows, lines = pl.pallas_call(
+        state, fields, rows, hits = pl.pallas_call(
             functools.partial(
                 main_kernel, n_slab, n_col, len(heart_scratch), len(torso_scratch)
             ),
@@ -690,26 +689,27 @@
                 jax.ShapeDtypeStruct((fields, nx, ny, nz), f32),
                 jax.ShapeDtypeStruct((3, SEGMENTS, nx, ny, nz), f32),
                 jax.ShapeDtypeStruct((n_slab, 4, LANES), f32),
-                jax.ShapeDtypeStruct((n_slab, 1, NARROW), f32),
+                jax.ShapeDtypeStruct((tx * ny, 2 * CAP * n_slab), jnp.bfloat16),
             ),
             in_specs=[hbm] * 4,
             out_specs=(vmem,) * 4,
             scratch_shapes=[
+                pltpu.VMEM((n_slab, 1, NARROW), f32),
                 *heart_scratch, *torso_scratch,
-                dma((3,)), dma((12,)), dma((PHASES, 12)), dma((2, 2)), regular, regular,
+                dma((3,)), dma((12,)), dma((PHASES, 12)), dma((2, 2)), regular,
             ],
             compiler_params=pltpu.CompilerParams(
                 collective_id=0, has_side_effects=True, vmem_limit_bytes=VMEM_LIMIT
             ),
         )(volume, epi_line, epi_dest, epi_target)
         return pl.pallas_call(
-            functools.partial(result_kernel, n_slab),
+            result_kernel,
             out_shape=jax.ShapeDtypeStruct(volume.shape, f32),
             in_specs=[vmem, vmem, vmem, vmem],
             out_specs=hbm,
             scratch_shapes=[pltpu.VMEM((SEGMENTS, nx, ny, nz), f32), dma((4,))],
             compiler_params=pltpu.CompilerParams(vmem_limit_bytes=VMEM_LIMIT),
-        )(state, fields, rows, lines)
+        )(state, fields, rows, hits)
 
     return jax.shard_map(
         on_device,

time: 31.4 us -> 30.9 us (0.984)
  the two profiles are of different devices: /device:TPU:80 before, /device:TPU:24 now
where the time goes in v5:
time: 30.9 us; the launch traced here: 30.6 us
  Pallas kernels  30.6 us (99%)
    pallas_call x1, Pallas kernels, on_device(): pl.pallas_call(functools.partial(main_kernel, n_slab, n_col, len(heart_sc...  29.4 us
    pallas_call x1, Pallas kernels, on_device(): pl.pallas_call(result_kernel, out_shape=jax.ShapeDtypeStruct(volume.shape...  1.16 us

profile of v5, /device:TPU:24, one launch (start us, length us, event | category | flops | bytes accessed | tf_op | source)
XLA Modules:
  0.0 30.6 jit_solution(11339903907218249948)
XLA Ops:
  0.0 29.4 %shard_map.46 = (f32[20,8,8,256]{3,2,1,0:T(8,128)S(1)}, f32[3,5,8,8,256]{4,3,2,1,0:T(8,128)S(1)}, f32[64,4,128]{2,1,0:T(4,128)S(1)}, bf16[320,256]{1,0:T(8,128)(2,1)S(1)}) custom-call(f32[1,20,8,8,256]{4,3,2,1,0:T(8,128)} %refs_0_.1, s32[1,1,64]{2,1,0:T(1,128)} %refs_1_.1, s32[1,1,64]{2,1,0:T(1,128)} %bitcast.1, s32[1,1,64]{2,1,0:T(1,128)} %refs_3_.1), custom_call_target="tpu_custom_call" | custom-call | tf_op jit(solution)/shard_map/pallas_call | solution.py:684
  29.4 1.2 %shard_map.47 = f32[1,20,8,8,256]{4,3,2,1,0:T(8,128)} custom-call(f32[20,8,8,256]{3,2,1,0:T(8,128)S(1)} %get-tuple-element.9.state, f32[3,5,8,8,256]{4,3,2,1,0:T(8,128)S(1)} %get-tuple-element.10.fields, f32[64,4,128]{2,1,0:T(4,128)S(1)} %get-tuple-element.11.rows, bf16[320,256]{1,0:T(8,128)(2,1)S(1)} %get-tuple-element.12.hits), custom_call_target="tpu_custom_call" | custom-call | tf_op jit(solution)/shard_map/pallas_call | solution.py:705

commit v6 on v5

--- a/solution.py
+++ b/solution.py
@@ -11,6 +11,8 @@
 STEPS = 4
 CAP = 2
 GATES = 18
+PARTS = 3
+CHUNK = GATES // PARTS
 LANES = 128
 NARROW = 8
 SEGMENTS = 5
@@ -71,8 +73,8 @@
             for i in range(N_RING)
         ]
 
-    def greet(self, others):
-        for here, there in self.met[4:] + others + self.met[:4]:
+    def greet(self, first=(), last=()):
+        for here, there in [*self.met[4:], *first, *self.met[:4], *last]:
 
             @pl.when(here)
             def _(there=there):
@@ -189,12 +191,13 @@
         current = sum(c * (volts * sums[c] - weighted[c]) for c in sums)
         pots[step + 1, x] = volts + sigma * flux - current
 
-    def first_moments(x, _):
-        later, later_weighted = 0.0, 0.0
-        for j in range(GATES):
-            part = state[1 + j, x] * float(gate_conduct[j] * gate_decay[j])
-            later += part
-            later_weighted += part * float(gate_reversal[j])
+    def first_moments(part, x, _):
+        later = moments[0, x] if part else 0.0
+        later_weighted = moments[1, x] if part else 0.0
+        for j in range(part * CHUNK, (part + 1) * CHUNK):
+            share = state[1 + j, x] * float(gate_conduct[j] * gate_decay[j])
+            later += share
+            later_weighted += share * float(gate_reversal[j])
         moments[0, x] = later
         moments[1, x] = later_weighted
         return 0
@@ -288,18 +291,21 @@
     def heart():
         loads = [
             load(vol.at[0, 0], pots.at[0], send_sem.at[4]),
-            load(vol.at[0, pl.ds(1, GATES + 1)], state.at[pl.ds(1, GATES + 1)], send_sem.at[5]),
-        ]
+        ]
+        for part in range(PARTS):
+            rows = pl.ds(1 + part * CHUNK, CHUNK + part // (PARTS - 1))
+            loads.append(load(vol.at[0, rows], state.at[rows], send_sem.at[5 + part]))
         metas = [
             load(src.at[0], meta.at[i], meta_sem.at[i])
             for i, src in enumerate((line_hbm, dest_hbm, target_hbm))
         ]
-        place_.greet(place_.across(1))
+        place_.greet(last=place_.across(1))
         loads[0].wait()
         place_.await_met()
         edges = send_edges(0)
-        loads[1].wait()
-        lax.fori_loop(0, nx, first_moments, 0, unroll=2)
+        for part in range(PARTS):
+            loads[1 + part].wait()
+            lax.fori_loop(0, nx, functools.partial(first_moments, part), 0, unroll=2)
         rest = send_rest(0)
 
         for copy in metas:
@@ -540,7 +546,7 @@
             others += [(at == 0, along(-1)), (at == ring_size - 1, along(1))]
         for k in sorted(range(2, ring_size - 1), key=lambda k: -min(k, ring_size - k)):
             others.append((slab >= 0, along(k)))
-        place_.greet(others)
+        place_.greet(first=others)
 
         hearts = place_.across(0)
         place_.await_met(others + hearts)

time: 30.9 us -> 30.7 us (level)
  no operation moved by 1% of the time
where the time goes in v6:
time: 30.7 us; the launch traced here: 30.4 us
  Pallas kernels  30.4 us (99%)
    pallas_call x1, Pallas kernels, on_device(): pl.pallas_call(functools.partial(main_kernel, n_slab, n_col, len(heart_sc...  29.3 us
    pallas_call x1, Pallas kernels, on_device(): pl.pallas_call(result_kernel, out_shape=jax.ShapeDtypeStruct(volume.shape...  1.16 us

profile of v6, /device:TPU:24, one launch (start us, length us, event | category | flops | bytes accessed | tf_op | source)
XLA Modules:
  0.0 30.4 jit_solution(6538111449704919879)
XLA Ops:
  0.0 29.3 %shard_map.46 = (f32[20,8,8,256]{3,2,1,0:T(8,128)S(1)}, f32[3,5,8,8,256]{4,3,2,1,0:T(8,128)S(1)}, f32[64,4,128]{2,1,0:T(4,128)S(1)}, bf16[320,256]{1,0:T(8,128)(2,1)S(1)}) custom-call(f32[1,20,8,8,256]{4,3,2,1,0:T(8,128)} %refs_0_.1, s32[1,1,64]{2,1,0:T(1,128)} %refs_1_.1, s32[1,1,64]{2,1,0:T(1,128)} %bitcast.1, s32[1,1,64]{2,1,0:T(1,128)} %refs_3_.1), custom_call_target="tpu_custom_call" | custom-call | tf_op jit(solution)/shard_map/pallas_call | solution.py:690
  29.3 1.2 %shard_map.47 = f32[1,20,8,8,256]{4,3,2,1,0:T(8,128)} custom-call(f32[20,8,8,256]{3,2,1,0:T(8,128)S(1)} %get-tuple-element.9.state, f32[3,5,8,8,256]{4,3,2,1,0:T(8,128)S(1)} %get-tuple-element.10.fields, f32[64,4,128]{2,1,0:T(4,128)S(1)} %get-tuple-element.11.rows, bf16[320,256]{1,0:T(8,128)(2,1)S(1)} %get-tuple-element.12.hits), custom_call_target="tpu_custom_call" | custom-call | tf_op jit(solution)/shard_map/pallas_call | solution.py:711
